TPU v7x, 256 devices: a whole 4x4x8 slice. The times are simulated.
256 devices in a mesh: cuts: 4 (over z_hi, core), member: 16 (over y, z_lo), grid: 4 (over x).
Axes of the slice: x: 4, y: 4, z: 8 (z_hi: 2, z_lo: 4; z = z_hi * 4 + z_lo), core: 2. Of those that a mesh axis runs over, the one named last changes fastest.
Arguments:
- hidden: bfloat16 [4, 16, 8192, 1024], P('cuts', 'member', 'grid'), may hold values from -6 to 6
- noise_seeds: int32 [16], P('member'), may hold values from 0 to 63
- noise_table: float32 [64, 1024], replicated, may hold values from -4 to 4
- inner_weight: bfloat16 [1024, 1024], replicated, may hold values from -0.1875 to 0.1875
- inner_bias: float32 [1024], replicated, may hold values from -3 to 3
- output_weight: bfloat16 [100, 1024], replicated, may hold values from -0.1875 to 0.1875
- output_bias: float32 [100], replicated, may hold values from -3 to 3
- state_bank: float32 [8, 100, 4, 16, 128], P(None, None, 'grid', 'member'), may hold values from -6 to 6
- ic_index: int32 [4], P('cuts'), may hold values from 0 to 7
- target_index: int32 [4], P('cuts'), may hold values from 0 to 7
- area_weight: float32 [4, 16, 128], P('grid', 'member'), may hold values from 0.1 to 1
Outputs:
- inner_weight_grad: float32 [1024, 1024], replicated
- inner_bias_grad: float32 [1024], replicated
- output_weight_grad: float32 [100, 1024], replicated
- output_bias_grad: float32 [100], replicated
- loss: float32 [], replicated
All inputs are finite; a program needn't handle non-finite values.
Results may differ from a plain program's by a relative error of at most 0.0037.
Values may be sent and summed in bfloat16 or wider, within the bound.
A program may use at most 128 MiB of HBM per device.

v0:
```python
import jax
import jax.numpy as jnp
from jax import lax
from jax.sharding import PartitionSpec as P

FAIR_ALPHA = 0.95


def body(
    hidden,
    noise_seeds,
    noise_table,
    inner_weight,
    inner_bias,
    output_weight,
    output_bias,
    state_bank,
    ic_index,
    target_index,
    area_weight,
):
    members_here = hidden.shape[1]
    points_here = hidden.shape[2]
    hidden_width = hidden.shape[3]
    variables = output_weight.shape[0]
    seed_ids = jnp.arange(noise_table.shape[0], dtype=jnp.int32)
    seeds_onehot = (noise_seeds[:, None] == seed_ids[None, :]).astype(jnp.float32)
    noise_rows = jnp.dot(
        seeds_onehot,
        noise_table,
        precision=lax.Precision.HIGHEST,
        preferred_element_type=jnp.float32,
    )
    noisy = (hidden[0].astype(jnp.float32) + noise_rows[:, None, :]).astype(jnp.bfloat16)
    noisy = noisy.reshape(members_here * points_here, hidden_width)
    pre_act = jnp.dot(noisy, inner_weight, preferred_element_type=jnp.float32) + inner_bias
    activation, gelu_back = jax.vjp(jax.nn.gelu, pre_act)
    activation = activation.astype(jnp.bfloat16)
    prediction = (
        lax.dot_general(
            output_weight, activation, (((1,), (1,)), ((), ())), preferred_element_type=jnp.float32
        )
        + output_bias[:, None]
    )
    prediction = prediction.reshape(variables, members_here, points_here)
    point_pred = lax.all_to_all(prediction, "member", split_axis=2, concat_axis=1, tiled=True)
    member_count = point_pred.shape[1]
    flat_bank = state_bank[:, :, 0, 0, :]
    ic_state = lax.dynamic_index_in_dim(flat_bank, ic_index[0], 0, keepdims=False)
    truth_field = lax.dynamic_index_in_dim(flat_bank, target_index[0], 0, keepdims=False)
    ensemble = point_pred + ic_state[:, None, :]
    point_weight = area_weight[0, 0]
    sample_count = lax.axis_size("cuts") * hidden.shape[0]
    total_points = lax.axis_size("grid") * points_here
    epsilon = (1.0 - FAIR_ALPHA) / member_count
    pair_scale = (1.0 - epsilon) / (member_count * (member_count - 1.0))
    errors = ensemble - truth_field[:, None, :]
    differences = ensemble[:, :, None, :] - ensemble[:, None, :, :]
    skill_sum = jnp.sum(jnp.abs(errors), axis=1)
    spread_sum = jnp.sum(jnp.abs(differences), axis=(1, 2))
    sign_sums = jnp.sum(jnp.sign(differences), axis=2)
    crps_field = skill_sum / member_count - 0.5 * pair_scale * spread_sum
    local_loss = jnp.sum(point_weight * crps_field) / (sample_count * total_points * variables)
    member_grad = (
        point_weight / sample_count * (jnp.sign(errors) / member_count - pair_scale * sign_sums)
    ).astype(jnp.bfloat16)
    returned = lax.all_to_all(member_grad, "member", split_axis=1, concat_axis=2, tiled=True)
    returned = returned.reshape(variables, members_here * points_here)
    grad_b2 = jnp.sum(returned.astype(jnp.float32), axis=1)
    grad_w2 = jnp.dot(returned, activation, preferred_element_type=jnp.float32)
    carried = lax.dot_general(
        returned, output_weight, (((0,), (0,)), ((), ())), preferred_element_type=jnp.float32
    )
    pre_grad = gelu_back(carried)[0].astype(jnp.bfloat16)
    grad_b1 = jnp.sum(pre_grad.astype(jnp.float32), axis=0)
    grad_w1 = lax.dot_general(
        noisy, pre_grad, (((0,), (0,)), ((), ())), preferred_element_type=jnp.float32
    )
    grad_w1, grad_b1, grad_w2, grad_b2, loss = lax.psum(
        (grad_w1, grad_b1, grad_w2, grad_b2, local_loss), ("cuts", "member", "grid")
    )
    return (grad_w1, grad_b1, grad_w2, grad_b2, loss)


def solution(mesh):
    return jax.shard_map(
        body,
        mesh=mesh,
        in_specs=(
            P("cuts", "member", "grid", None),
            P("member"),
            P(),
            P(),
            P(),
            P(),
            P(),
            P(None, None, "grid", "member", None),
            P("cuts"),
            P("cuts"),
            P("grid", "member", None),
        ),
        out_specs=(P(), P(), P(), P(), P()),
        check_vma=False,
    )
```

profile of v0, /device:TPU:1, one launch (start us, length us, event | category | flops | bytes accessed | tf_op | source)
XLA Modules:
  0.0 389.7 jit_solution(8578856110412567470)
XLA Ops:
  8.0 1.2 fusion.15
  9.2 11.4 %multiply_convert_fusion = (bf16[2048,1024]{1,0:T(8,128)(2,1)S(1)}, f32[2048,1024]{1,0:T(8,128)}) fusion(f32[1024]{0:T(1024)} %param.15, bf16[1024,1024]{1,0:T(8,128)(2,1)S(1)} %copy-done, bf16[1,1,2048,1024]{3,2,1,0:T(8,128)(2,1)} %param.11, f32[1024]{0:T(1024)S(1)} %bitcast.54), kind=kOutput, calls=%fused_computation.16 | convolution fusion | flops 4322230272 | bytes 18882560 | tf_op jit(solution)/shard_map/dot_general | solution.py:36
  20.6 2.0 copy-done.1
  22.6 1.4 fusion.14
  24.1 1.9 copy.23
  26.0 9.2 %all-to-all-start = ((f32[100,1,2048]{0,1,2:T(1,128)}), f32[100,1,2048]{0,1,2:T(1,128)S(1)}, u32[]{:S(2)}, u32[]{:S(2)}) async-start(f32[100,1,2048]{0,1,2:T(1,128)} %copy.23), calls=%async_computation | async-start | bytes 2097152 | tf_op jit(solution)/shard_map/all_to_all | solution.py:46
  35.2 0.2 all-reduce.4.cloned.1.call-start
  36.7 0.9 constant_dynamic-slice_fusion.1
  37.6 24.5 %all-to-all-done = f32[100,1,2048]{0,1,2:T(1,128)S(1)} async-done(((f32[100,1,2048]{0,1,2:T(1,128)}), f32[100,1,2048]{0,1,2:T(1,128)S(1)}, u32[]{:S(2)}, u32[]{:S(2)}) %all-to-all-start) | async-done | bytes 819232 | tf_op jit(solution)/shard_map/all_to_all | solution.py:46
  62.2 1.4 copy.27
  63.5 1.6 abs_reduce_fusion
  65.1 7.5 %fusion.1 = (f32[100,128]{1,0:T(8,128)S(1)}, f32[100,16,128]{2,1,0:T(8,128)S(1)}) fusion(f32[100,16,128]{2,1,0:T(8,128)S(1)} %get-tuple-element.13), kind=kLoop, calls=%fused_computation.3 | loop fusion | flops 16166400 | bytes 1689600 | tf_op jit(solution)/shard_map/reduce_sum | solution.py:60
  72.6 0.4 multiply_convert_fusion.1
  73.1 17.8 %all_to_all.21 = bf16[100,16,128]{2,0,1:T(8,128)(2,1)S(1)} all-to-all(bf16[100,16,128]{2,0,1:T(8,128)(2,1)S(1)} %copy.25), channel_id=1, replica_groups=mesh['cuts'=4,'member'=16,'grid'=4] {'member'}, dimensions={1} | all-to-all | bytes 819200 | tf_op jit(solution)/shard_map/all_to_all | solution.py:67
  91.1 0.1 copy.30
  91.2 1.5 fusion.20
  92.7 9.0 %convert_reduce_fusion = (f32[1024]{0:T(1024)S(1)}, bf16[2048,1024]{1,0:T(8,128)(2,1)S(1)}) fusion(f32[2048,1024]{1,0:T(8,128)} %get-tuple-element.17, f32[1024]{0:T(1024)S(1)} %copy-done.8, bf16[100,2048]{1,0:T(8,128)(2,1)S(1)} %bitcast.49, bf16[100,1024]{1,0:T(8,128)(2,1)S(1)} %copy-done.4), kind=kOutput, calls=%fused_computation.15 | convolution fusion | flops 467663872 | bytes 13205504 | tf_op jit(solution)/shard_map/dot_general | solution.py:71
  101.7 6.1 %fusion.10 = f32[1024,1024]{1,0:T(8,128)} fusion(bf16[2048,1024]{1,0:T(8,128)(2,1)S(1)} %get-tuple-element.19, bf16[1,1,2048,1024]{3,2,1,0:T(8,128)(2,1)S(1)} %copy-done.7, f32[1024]{0:T(1024)S(1)} %bitcast.55), kind=kOutput, calls=%fused_computation.17 | convolution fusion | flops 4301258752 | bytes 12587008 | tf_op jit(solution)/shard_map/dot_general | solution.py:76
  107.8 0.6 multiply_reduce_fusion
  109.1 0.1 convert_reduce_fusion.1
  109.2 76.3 %all-reduce = (f32[1024]{0:T(1024)}, f32[100]{0:T(128)}, f32[]{:T(128)}) all-reduce(f32[1024]{0:T(1024)S(1)} %get-tuple-element.18, f32[100]{0:T(128)S(1)} %convert_reduce_fusion.1, f32[]{:T(128)S(6)} %div.27), channel_id=1, replica_groups=mesh['cuts'=4,'member'=16,'grid'=4] {'cuts','member','grid'}, use_global_device_ids=true, to_apply=%region_3.4 | all-reduce | flops 1125 | bytes 9000 | tf_op jit(solution)/shard_map/psum | solution.py:79
  185.5 191.8 %all-reduce.4.cloned.1.call-done = (f32[1024,1024]{1,0:T(8,128)}, f32[100,1024]{1,0:T(8,128)}) async-done(((f32[1024,1024]{1,0:T(8,128)}, f32[100,1024]{1,0:T(8,128)}), (f32[1024,1024]{1,0:T(8,128)}, f32[100,1024]{1,0:T(8,128)})) %all-reduce.4.cloned.1.call-update) | async-done | bytes 4603920 | tf_op jit(solution)/shard_map/psum | solution.py:79
  377.3 4.8 %copy.40 = f32[1024,1024]{1,0:T(8,128)} copy(f32[1024,1024]{1,0:T(8,128)} %get-tuple-element.20) | data formatting | bytes 8388608
  382.1 0.8 copy.41
  (24 shorter events, 0.3 us)
Async XLA Ops:
  7.2 2.0 copy-start
  9.1 13.5 %copy-start.4 = (bf16[100,1024]{1,0:T(8,128)(2,1)S(1)}, bf16[100,1024]{1,0:T(8,128)(2,1)}, u32[]{:S(2)}) copy-start(bf16[100,1024]{1,0:T(8,128)(2,1)} %param.16) | copy-start | bytes 614404
  9.1 13.5 %copy-start.5 = (f32[100]{0:T(128)S(1)}, f32[100]{0:T(128)}, u32[]{:S(2)}) copy-start(f32[100]{0:T(128)} %param.17) | copy-start | bytes 1204
  20.6 2.0 copy-start.1
  20.6 17.0 %copy-start.6 = (f32[1,1,128]{2,1,0:T(1,128)S(1)}, f32[1,1,128]{2,1,0:T(1,128)}, u32[]{:S(2)}) copy-start(f32[1,1,128]{2,1,0:T(1,128)} %param.21) | copy-start | bytes 1540
  26.0 36.2 %all-to-all-start = ((f32[100,1,2048]{0,1,2:T(1,128)}), f32[100,1,2048]{0,1,2:T(1,128)S(1)}, u32[]{:S(2)}, u32[]{:S(2)}) async-start(f32[100,1,2048]{0,1,2:T(1,128)} %copy.23), calls=%async_computation | async-start | bytes 2097152 | tf_op jit(solution)/shard_map/all_to_all | solution.py:46
  35.2 342.1 %all-reduce.4.cloned.1.call-start = ((), (), s32[]{:S(2)}) async-start(), calls=%async_computation.2 | async-start | bytes 9240576 | tf_op jit(solution)/shard_map/psum | solution.py:79
  62.2 30.5 %copy-start.8 = (f32[1024]{0:T(1024)S(1)}, f32[1024]{0:T(1024)}, u32[]{:S(2)}) copy-start(f32[1024]{0:T(1024)} %param.15) | copy-start | bytes 12292
  63.5 27.6 %copy-start.2 = (bf16[2048,1024]{1,0:T(8,128)(2,1)S(1)}, bf16[2048,1024]{1,0:T(8,128)(2,1)}, u32[]{:S(2)}) copy-start(bf16[2048,1024]{1,0:T(8,128)(2,1)} %copy-done.1) | copy-start | bytes 12582916
  92.7 9.0 %copy-start.7 = (bf16[1,1,2048,1024]{3,2,1,0:T(8,128)(2,1)S(1)}, bf16[1,1,2048,1024]{3,2,1,0:T(8,128)(2,1)}, u32[]{:S(2)}) copy-start(bf16[1,1,2048,1024]{3,2,1,0:T(8,128)(2,1)} %param.11) | copy-start | bytes 12582916
  377.3 4.8 %copy-start.3 = (f32[100,1024]{1,0:T(8,128)S(1)}, f32[100,1024]{1,0:T(8,128)}, u32[]{:S(2)}) copy-start(f32[100,1024]{1,0:T(8,128)} %get-tuple-element.22) | copy-start | bytes 1228804
Sparse Core Ops, SparseCore 0:
  107.9 269.2 all-reduce.3
where the time goes:
time: 391 us; the launch traced here: 390 us
  waiting for transfers between devices  216 us (55%)
  blocking collectives  94.1 us (24%)
  matrix products  30.6 us (8%)
  between operations  16.9 us (4%)
  local copies, waits for them, and re-layouts  12.1 us (3%)
  other arithmetic  10.2 us (3%)
  starting transfers between devices  9.41 us (2%)
    psum x1, waiting for transfers between devices, body(): lax.psum((grad_w1, grad_b1, grad_w2, grad_b2, local_loss), ('cuts', 'memb...  192 us
    psum x1, blocking collectives, body(): lax.psum((grad_w1, grad_b1, grad_w2, grad_b2, local_loss), ('cuts', 'memb...  76.3 us
    all_to_all x1, waiting for transfers between devices, body(): lax.all_to_all(prediction, 'member', split_axis=2, concat_axis=1, tiled=T...  24.5 us
    all_to_all x1, blocking collectives, body(): lax.all_to_all(member_grad, 'member', split_axis=1, concat_axis=2, tiled=...  17.8 us
    dot_general x1, matrix products, body(): jnp.dot(noisy, inner_weight, preferred_element_type=jnp.float32)  11.4 us
    all_to_all x1, starting transfers between devices, body(): lax.all_to_all(prediction, 'member', split_axis=2, concat_axis=1, tiled=T...  9.19 us
    dot_general x1, matrix products, body(): lax.dot_general(returned, output_weight, (((0,), (0,)), ((), ())), prefer...  8.96 us
  transfers between devices with their start and end apart: 2, of which 2 were waited for; matrix products, arithmetic and copies ran while one was open for 0% of the time, Pallas kernels for 0%

commit v1 on v0

--- a/solution.py
+++ b/solution.py
@@ -1,9 +1,283 @@
 import jax
 import jax.numpy as jnp
 from jax import lax
+from jax.experimental import pallas as pl
+from jax.experimental.pallas import tpu as pltpu
 from jax.sharding import PartitionSpec as P
 
 FAIR_ALPHA = 0.95
+MESH = pl.DeviceIdType.MESH
+BLOCKS = 4
+
+
+def place():
+    cuts, member, x = lax.axis_index("cuts"), lax.axis_index("member"), lax.axis_index("grid")
+    core, z_hi = lax.rem(cuts, 2), lax.div(cuts, 2)
+    y, z_lo = lax.div(member, 4), lax.rem(member, 4)
+    return core, x, y, z_hi * 4 + z_lo
+
+
+def device(core, x, y, z):
+    return (lax.div(z, 4) * 2 + core, y * 4 + lax.rem(z, 4), x)
+
+
+def partners(spot):
+    core, x, y, z = spot
+    found = [device(1 - core, x, y, z)]
+    found += [device(core, lax.rem(x + k, 4), y, z) for k in range(1, 4)]
+    found += [device(core, x, lax.rem(y + k, 4), z) for k in range(1, 4)]
+    found += [device(core, x, y, lax.rem(z + k, 8)) for k in range(1, 8)]
+    return found
+
+
+def greet(devices):
+    barrier = pltpu.get_barrier_semaphore()
+    for one in devices:
+        pl.semaphore_signal(barrier, inc=1, device_id=one, device_id_type=MESH)
+    pl.semaphore_wait(barrier, len(devices))
+
+
+class Total:
+    def __init__(self, spot, acc, out, pair, part1, got1, part2, got2, ztx, zrx, ztile, zall, sems):
+        self.spot, self.acc, self.out = spot, acc, out
+        self.pair, self.part1, self.got1, self.part2, self.got2 = pair, part1, got1, part2, got2
+        self.ztx, self.zrx, self.ztile, self.zall = ztx, zrx, ztile, zall
+        (self.pair_s, self.pair_r, self.s1, self.r1, self.s2, self.r2, self.zs, self.zr,
+         self.gz_s, self.gz_r, self.g2_s, self.g2_r, self.g1_s, self.g1_r, self.gp_s, self.gp_r) = sems
+
+    def axes(self, block):
+        _, x, y, _ = self.spot
+        return (x, y) if block % 2 == 0 else (y, x)
+
+    def along(self, block, phase, k):
+        core, x, y, z = self.spot
+        if (block + phase) % 2 == 0:
+            return device(core, lax.rem(x + k, 4), y, z)
+        return device(core, x, lax.rem(y + k, 4), z)
+
+    def columns(self, block, core):
+        return pl.ds(pl.multiple_of(block * 256 + core * 128, 128), 128)
+
+    def copy(self, src, dst, send, recv, target):
+        return pltpu.make_async_remote_copy(
+            src_ref=src, dst_ref=dst, send_sem=send, recv_sem=recv, device_id=target, device_id_type=MESH
+        )
+
+    def pair_copy(self, block):
+        core, x, y, z = self.spot
+        return self.copy(
+            self.acc.at[:, self.columns(block, 1 - core)], self.pair.at[block],
+            self.pair_s.at[block], self.pair_r.at[block], device(1 - core, x, y, z),
+        )
+
+    def pair_start(self, block):
+        self.pair_copy(block).start()
+
+    def pair_end(self, block):
+        core = self.spot[0]
+        self.pair_copy(block).wait()
+        self.part1[block] = self.acc[:, self.columns(block, core)] + self.pair[block]
+
+    def first_copy(self, block, k):
+        mine = self.axes(block)[0]
+        rows = pl.ds(pl.multiple_of(lax.rem(mine + k, 4) * 288, 8), 288)
+        return self.copy(
+            self.part1.at[block, rows], self.got1.at[block, k - 1],
+            self.s1.at[block, k - 1], self.r1.at[block, k - 1], self.along(block, 0, k),
+        )
+
+    def first_start(self, block):
+        for k in range(1, 4):
+            self.first_copy(block, k).start()
+
+    def first_end(self, block):
+        mine = self.axes(block)[0]
+        for k in range(1, 4):
+            self.first_copy(block, k).wait()
+        own = self.part1[block, pl.ds(pl.multiple_of(mine * 288, 8), 288)]
+        self.part2[block] = (own + self.got1[block, 0]) + (self.got1[block, 1] + self.got1[block, 2])
+
+    def second_copy(self, block, k):
+        mine = self.axes(block)[1]
+        rows = pl.ds(pl.multiple_of(lax.rem(mine + k, 4) * 72, 8), 72)
+        return self.copy(
+            self.part2.at[block, rows], self.got2.at[block, k - 1],
+            self.s2.at[block, k - 1], self.r2.at[block, k - 1], self.along(block, 1, k),
+        )
+
+    def second_start(self, block):
+        for k in range(1, 4):
+            self.second_copy(block, k).start()
+
+    def second_end(self, block):
+        mine = self.axes(block)[1]
+        for k in range(1, 4):
+            self.second_copy(block, k).wait()
+        own = self.part2[block, pl.ds(pl.multiple_of(mine * 72, 8), 72)]
+        total = (own + self.got2[block, 0]) + (self.got2[block, 1] + self.got2[block, 2])
+        for other in range(8):
+            self.ztx[other, block, 0:8] = total[8 * other : 8 * other + 8]
+            self.ztx[other, block, 8:16] = total[64:72]
+
+    def z_copy(self, k):
+        core, x, y, z = self.spot
+        other = lax.rem(z + k, 8)
+        return self.copy(
+            self.ztx.at[other], self.zrx.at[z], self.zs.at[k - 1], self.zr.at[k - 1], device(core, x, y, other)
+        )
+
+    def z_start(self):
+        z = self.spot[3]
+        for k in range(1, 8):
+            self.z_copy(k).start()
+        self.zrx[z] = self.ztx[z]
+
+    def z_end(self):
+        core, x, y, z = self.spot
+        for k in range(1, 8):
+            self.z_copy(k).wait_send()
+            origin = lax.rem(z + 8 - k, 8)
+            self.copy(
+                self.ztx.at[z], self.zrx.at[origin], self.zs.at[k - 1], self.zr.at[k - 1], device(core, x, y, origin)
+            ).wait_recv()
+        total = self.zrx[0]
+        for other in range(1, 8):
+            total = total + self.zrx[other]
+        self.ztile[...] = total
+
+    def gather_z_copy(self, k, spot_z):
+        core, x, y, z = self.spot
+        return self.copy(
+            self.ztile.at[:, 0:8], self.zall.at[spot_z], self.gz_s.at[k - 1], self.gz_r.at[k - 1],
+            device(core, x, y, lax.rem(z + k, 8)),
+        )
+
+    def gather_z_start(self):
+        z = self.spot[3]
+        for k in range(1, 8):
+            self.gather_z_copy(k, z).start()
+        self.zall[z] = self.ztile[:, 0:8]
+
+    def chunk(self, block):
+        one, two = self.axes(block)
+        return one * 288 + two * 72
+
+    def gather_z_end(self):
+        core, _, _, z = self.spot
+        for k in range(1, 8):
+            self.gather_z_copy(k, z).wait_send()
+            self.gather_z_copy(k, lax.rem(z + 8 - k, 8)).wait_recv()
+        for block in range(BLOCKS):
+            base = self.chunk(block)
+            columns = self.columns(block, core)
+            for other in range(8):
+                self.out[pl.ds(pl.multiple_of(base + 8 * other, 8), 8), columns] = self.zall[other, block]
+            self.out[pl.ds(pl.multiple_of(base + 64, 8), 8), columns] = self.ztile[block, 8:16]
+
+    def gather_copy(self, block, phase, k, sender):
+        core = self.spot[0]
+        one, two = self.axes(block)
+        if phase == 1:
+            if sender:
+                two = lax.rem(two + 4 - k, 4)
+            rows, size, send, recv = one * 288 + two * 72, 72, self.g2_s, self.g2_r
+        else:
+            if sender:
+                one = lax.rem(one + 4 - k, 4)
+            rows, size, send, recv = one * 288, 288, self.g1_s, self.g1_r
+        spot = self.out.at[pl.ds(pl.multiple_of(rows, 8), size), self.columns(block, core)]
+        return self.copy(spot, spot, send.at[block, k - 1], recv.at[block, k - 1], self.along(block, phase, k))
+
+    def gather_start(self, block, phase):
+        for k in range(1, 4):
+            self.gather_copy(block, phase, k, False).start()
+
+    def gather_end(self, block, phase):
+        for k in range(1, 4):
+            self.gather_copy(block, phase, k, False).wait_send()
+            self.gather_copy(block, phase, k, True).wait_recv()
+
+    def gather_pair_copy(self, block, core_of):
+        core, x, y, z = self.spot
+        spot = self.out.at[:, self.columns(block, core_of)]
+        return self.copy(spot, spot, self.gp_s.at[block], self.gp_r.at[block], device(1 - core, x, y, z))
+
+    def gather_pair_start(self, block):
+        self.gather_pair_copy(block, self.spot[0]).start()
+
+    def gather_pair_end(self, block):
+        self.gather_pair_copy(block, self.spot[0]).wait_send()
+        self.gather_pair_copy(block, 1 - self.spot[0]).wait_recv()
+
+    def finish(self):
+        blocks = range(BLOCKS)
+        self.z_start()
+        self.z_end()
+        self.gather_z_start()
+        self.gather_z_end()
+        for b in blocks:
+            self.gather_start(b, 1)
+        for b in blocks:
+            self.gather_end(b, 1)
+            self.gather_start(b, 0)
+        for b in blocks:
+            self.gather_end(b, 0)
+            self.gather_pair_start(b)
+        for b in blocks:
+            self.gather_pair_end(b)
+
+
+def total_scratch():
+    f32 = jnp.float32
+    dma = pltpu.SemaphoreType.DMA
+    buffers = [
+        pltpu.VMEM((BLOCKS, 1152, 128), f32),
+        pltpu.VMEM((BLOCKS, 1152, 128), f32),
+        pltpu.VMEM((BLOCKS, 3, 288, 128), f32),
+        pltpu.VMEM((BLOCKS, 288, 128), f32),
+        pltpu.VMEM((BLOCKS, 3, 72, 128), f32),
+        pltpu.VMEM((8, BLOCKS, 16, 128), f32),
+        pltpu.VMEM((8, BLOCKS, 16, 128), f32),
+        pltpu.VMEM((BLOCKS, 16, 128), f32),
+        pltpu.VMEM((8, BLOCKS, 8, 128), f32),
+    ]
+    shapes = [(BLOCKS,), (BLOCKS, 3), (BLOCKS, 3), (7,), (7,), (BLOCKS, 3), (BLOCKS, 3), (BLOCKS,)]
+    sems = []
+    for shape in shapes:
+        sems += [dma(shape), dma(shape)]
+    return buffers, sems
+
+
+def total_kernel(acc, out, *scratch):
+    spot = place()
+    greet(partners(spot))
+    job = Total(spot, acc, out, *scratch[:9], scratch[9:])
+    blocks = range(BLOCKS)
+    for b in blocks:
+        job.pair_start(b)
+    for b in blocks:
+        job.pair_end(b)
+        job.first_start(b)
+    for b in blocks:
+        job.first_end(b)
+        job.second_start(b)
+    for b in blocks:
+        job.second_end(b)
+    job.finish()
+
+
+def all_total(acc):
+    buffers, sems = total_scratch()
+    return pl.pallas_call(
+        total_kernel,
+        out_shape=jax.ShapeDtypeStruct(acc.shape, jnp.float32),
+        in_specs=[pl.BlockSpec(memory_space=pltpu.VMEM)],
+        out_specs=pl.BlockSpec(memory_space=pltpu.VMEM),
+        scratch_shapes=buffers + sems,
+        compiler_params=pltpu.CompilerParams(
+            collective_id=0, has_side_effects=True, vmem_limit_bytes=48 * 1024 * 1024
+        ),
+    )(acc)
 
 
 def body(
@@ -76,10 +350,20 @@
     grad_w1 = lax.dot_general(
         noisy, pre_grad, (((0,), (0,)), ((), ())), preferred_element_type=jnp.float32
     )
-    grad_w1, grad_b1, grad_w2, grad_b2, loss = lax.psum(
-        (grad_w1, grad_b1, grad_w2, grad_b2, local_loss), ("cuts", "member", "grid")
-    )
-    return (grad_w1, grad_b1, grad_w2, grad_b2, loss)
+    rows = jnp.zeros((28, hidden_width), jnp.float32)
+    rows = rows.at[0].set(grad_b1).at[1, :variables].set(grad_b2).at[1, variables].set(local_loss)
+    second = jnp.concatenate([grad_w2, rows], axis=0)
+    packed = jnp.concatenate([grad_w1.reshape(4, 4, 64, hidden_width), second.reshape(4, 4, 8, hidden_width)], axis=2)
+    summed = all_total(packed.reshape(1152, hidden_width)).reshape(4, 4, 72, hidden_width)
+    grad_w1 = summed[:, :, :64].reshape(hidden_width, hidden_width)
+    second = summed[:, :, 64:].reshape(128, hidden_width)
+    return (
+        grad_w1,
+        second[variables],
+        second[:variables],
+        second[variables + 1, :variables],
+        second[variables + 1, variables],
+    )
 
 
 def solution(mesh):

time: 391 us -> 187 us (0.48)
  waiting for transfers between devices: 216 us -> 37.1 us
  blocking collectives: 94.1 us -> 0 us
  Pallas kernels: 0 us -> 66.6 us
  between operations: 16.9 us -> 3.62 us
  other arithmetic: 10.2 us -> 17.9 us
  local copies, waits for them, and re-layouts: 12.1 us -> 19.2 us
  starting transfers between devices: 9.41 us -> 13.6 us
    psum x1 -> x0, waiting for transfers between devices: 192 us -> none  [body(): lax.psum((grad_w1, grad_b1, grad_w2, grad_b2, local_loss), ('cuts', 'memb...]
    psum x1 -> x0, blocking collectives: 76.3 us -> none  [body(): lax.psum((grad_w1, grad_b1, grad_w2, grad_b2, local_loss), ('cuts', 'memb...]
    pallas_call x0 -> x1, Pallas kernels: none -> 66.6 us  [all_total(): pl.pallas_call(total_kernel, out_shape=jax.ShapeDtypeStruct(acc.shape, jn...]
    all_to_all x1 -> x0, blocking collectives: 17.8 us -> none  [body(): lax.all_to_all(member_grad, 'member', split_axis=1, concat_axis=2, tiled=...]
    all_to_all x0 -> x1, waiting for transfers between devices: none -> 12.3 us  [body(): lax.all_to_all(member_grad, 'member', split_axis=1, concat_axis=2, tiled=...]
    concatenate x0 -> x2, other arithmetic: none -> 5.07 us  [the longest x1 5.03 us: body(): jnp.concatenate([grad_w1.reshape(4, 4, 64, hidden_width), second.reshape(...]
    slice x0 -> x5, local copies, waits for them, and re-layouts: none -> 4.6 us  [the longest x1 2.6 us: body(): grad_w1 = summed[:, :, :64].reshape(hidden_width, hidden_width)]
    all_to_all x0 -> x1, starting transfers between devices: none -> 4.41 us  [body(): lax.all_to_all(member_grad, 'member', split_axis=1, concat_axis=2, tiled=...]
  transfers between devices with their start and end apart: 2 -> 2, of which waited for: 2 -> 2; matrix products, arithmetic and copies ran while one was open for 0% -> 1% of each run, Pallas kernels for 0% -> 0%
where the time goes in v1:
time: 187 us
  Pallas kernels  66.6 us (36%)
  waiting for transfers between devices  37.1 us (20%)
  matrix products  28.6 us (15%)
  local copies, waits for them, and re-layouts  19.2 us (10%)
  other arithmetic  17.9 us (10%)
  starting transfers between devices  13.6 us (7%)
  between operations  3.62 us (2%)
    pallas_call x1, Pallas kernels, all_total(): pl.pallas_call(total_kernel, out_shape=jax.ShapeDtypeStruct(acc.shape, jn...  66.6 us
    all_to_all x1, waiting for transfers between devices, body(): lax.all_to_all(prediction, 'member', split_axis=2, concat_axis=1, tiled=T...  24.8 us
    all_to_all x1, waiting for transfers between devices, body(): lax.all_to_all(member_grad, 'member', split_axis=1, concat_axis=2, tiled=...  12.3 us
    all_to_all x1, starting transfers between devices, body(): lax.all_to_all(prediction, 'member', split_axis=2, concat_axis=1, tiled=T...  9.2 us
    dot_general x1, matrix products, body(): jnp.dot(noisy, inner_weight, preferred_element_type=jnp.float32)  9.02 us
    dot_general x1, matrix products, body(): lax.dot_general(returned, output_weight, (((0,), (0,)), ((), ())), prefer...  8.97 us
    unnamed x23, local copies, waits for them, and re-layouts  8.64 us
    reduce_sum x1, other arithmetic, body(): spread_sum = jnp.sum(jnp.abs(differences), axis=(1, 2))  7.31 us
  transfers between devices with their start and end apart: 2, of which 2 were waited for; matrix products, arithmetic and copies ran while one was open for 1% of the time, Pallas kernels for 0%

profile of v1, /device:TPU:1, one launch (start us, length us, event | category | flops | bytes accessed | tf_op | source)
XLA Modules:
  0.0 186.7 jit_solution(9205638816322650878)
XLA Ops:
  1.5 6.4 %copy.27 = bf16[1,1,2048,1024]{2,3,1,0:T(8,128)(2,1)} copy(bf16[1,1,2048,1024]{3,2,1,0:T(8,128)(2,1)} %param.17) | data formatting | bytes 8388608 | tf_op args[0]
  8.1 2.9 %fusion.9 = bf16[2048,1024]{0,1:T(8,128)(2,1)S(1)} fusion(bf16[1,1,2048,1024]{2,3,1,0:T(8,128)(2,1)} %copy.27, f32[1024]{0:T(1024)S(1)} %bitcast.81), kind=kLoop, calls=%fused_computation.14 | loop fusion | flops 6291456 | bytes 8392704 | tf_op jit(solution)/shard_map/convert_element_type | solution.py:308
  11.1 9.0 %multiply_convert_fusion = (bf16[2048,1024]{1,0:T(8,128)(2,1)S(1)}, f32[2048,1024]{1,0:T(8,128)}) fusion(f32[1024]{0:T(1024)S(1)} %copy-done.8, bf16[2048,1024]{0,1:T(8,128)(2,1)S(1)} %fusion.9, bf16[1024,1024]{1,0:T(8,128)(2,1)S(1)} %copy-done), kind=kOutput, calls=%fused_computation.16 | convolution fusion | flops 4315938816 | bytes 18878464 | tf_op jit(solution)/shard_map/dot_general | solution.py:310
  20.1 2.0 %copy-done.1 = bf16[2048,1024]{1,0:T(8,128)(2,1)} copy-done((bf16[2048,1024]{1,0:T(8,128)(2,1)}, bf16[2048,1024]{1,0:T(8,128)(2,1)S(1)}, u32[]{:S(2)}) %copy-start.1) | copy-done | bytes 4194328
  22.1 1.5 fusion.12
  23.6 1.9 %copy.28 = f32[100,1,2048]{0,1,2:T(1,128)} copy(f32[100,1,2048]{2,0,1:T(8,128)S(1)} %fusion.12) | data formatting | bytes 1638400 | tf_op jit(solution)/shard_map/reshape | solution.py:319
  25.5 9.2 %all-to-all-start = ((f32[100,1,2048]{0,1,2:T(1,128)}), f32[100,1,2048]{0,1,2:T(1,128)S(1)}, u32[]{:S(2)}, u32[]{:S(2)}) async-start(f32[100,1,2048]{0,1,2:T(1,128)} %copy.28), calls=%async_computation | async-start | bytes 2097152 | tf_op jit(solution)/shard_map/all_to_all | solution.py:320
  36.0 0.9 constant_dynamic-slice_fusion.1
  37.0 24.8 %all-to-all-done = f32[100,1,2048]{0,1,2:T(1,128)S(1)} async-done(((f32[100,1,2048]{0,1,2:T(1,128)}), f32[100,1,2048]{0,1,2:T(1,128)S(1)}, u32[]{:S(2)}, u32[]{:S(2)}) %all-to-all-start) | async-done | bytes 819232 | tf_op jit(solution)/shard_map/all_to_all | solution.py:320
  61.7 1.4 copy.33
  63.1 1.4 abs_reduce_fusion
  64.5 7.3 %fusion.1 = (f32[100,128]{1,0:T(8,128)S(1)}, f32[100,16,128]{2,1,0:T(8,128)S(1)}) fusion(f32[100,16,128]{2,1,0:T(8,128)S(1)} %get-tuple-element.44), kind=kLoop, calls=%fused_computation.3 | loop fusion | flops 16166400 | bytes 1689600 | tf_op jit(solution)/shard_map/reduce_sum | solution.py:334
  72.2 0.9 copy.30
  73.1 4.4 %all-to-all-start.1 = ((bf16[100,16,128]{2,0,1:T(8,128)(2,1)}), bf16[100,16,128]{2,0,1:T(8,128)(2,1)S(1)}, u32[]{:S(2)}, u32[]{:S(2)}) async-start(bf16[100,16,128]{2,0,1:T(8,128)(2,1)} %copy.30), calls=%async_computation.1 | async-start | bytes 851968 | tf_op jit(solution)/shard_map/all_to_all | solution.py:341
  77.5 0.6 multiply_reduce_fusion
  78.8 12.3 %all-to-all-done.1 = bf16[100,16,128]{2,0,1:T(8,128)(2,1)S(1)} async-done(((bf16[100,16,128]{2,0,1:T(8,128)(2,1)}), bf16[100,16,128]{2,0,1:T(8,128)(2,1)S(1)}, u32[]{:S(2)}, u32[]{:S(2)}) %all-to-all-start.1) | async-done | bytes 409632 | tf_op jit(solution)/shard_map/all_to_all | solution.py:341
  91.3 2.9 %fusion.18 = f32[100,1024]{1,0:T(8,128)S(1)} fusion(bf16[100,2048]{1,0:T(8,128)(2,1)S(1)} %bitcast.75, bf16[2048,1024]{1,0:T(8,128)(2,1)} %copy-done.1), kind=kOutput, calls=%fused_computation.39 | convolution fusion | flops 419430400 | bytes 5013504 | tf_op jit(solution)/shard_map/dot_general | solution.py:344
  94.3 9.0 %convert_reduce_fusion = (f32[1024]{0:T(1024)S(1)}, bf16[2048,1024]{1,0:T(8,128)(2,1)S(1)}) fusion(f32[2048,1024]{1,0:T(8,128)} %get-tuple-element.48, f32[1024]{0:T(1024)S(1)} %copy-done.8, bf16[100,2048]{1,0:T(8,128)(2,1)S(1)} %bitcast.76, bf16[100,1024]{1,0:T(8,128)(2,1)S(1)} %copy-done.5), kind=kOutput, calls=%fused_computation.15 | convolution fusion | flops 467663872 | bytes 13205504 | tf_op jit(solution)/shard_map/dot_general | solution.py:345
  103.3 6.0 %fusion.10 = f32[4,4,64,1024]{3,2,1,0:T(8,128)} fusion(bf16[4,4,64,2048]{3,2,1,0:T(8,128)(2,1)S(1)} %bitcast.69, bf16[2048,1024]{1,0:T(8,128)(2,1)S(1)} %get-tuple-element.50), kind=kOutput, calls=%fused_computation.18 | convolution fusion | flops 4294967296 | bytes 12582912 | tf_op jit(solution)/shard_map/dot_general | solution.py:350
  109.9 5.0 %pad_maximum_fusion = f32[4,4,72,1024]{3,2,1,0:T(8,128)} fusion(f32[4,4,8,1024]{3,2,1,0:T(8,128)S(1)} %bitcast.70, f32[4,4,64,1024]{3,2,1,0:T(8,128)} %fusion.10), kind=kLoop, calls=%fused_computation.17 | loop fusion | flops 1179648 | bytes 9437184 | tf_op jit(solution)/shard_map/concatenate | solution.py:356
  114.9 66.6 %shard_map.146 = f32[1152,1024]{1,0:T(8,128)S(1)} custom-call(f32[1152,1024]{1,0:T(8,128)} %bitcast.66), custom_call_target="tpu_custom_call" | custom-call | tf_op jit(solution)/shard_map/pallas_call | solution.py:271
  181.6 2.6 %slice.76 = f32[4,4,64,1024]{3,2,1,0:T(8,128)} slice(f32[4,4,72,1024]{3,2,1,0:T(8,128)S(1)} %bitcast.65), slice={[0:4], [0:4], [0:64], [0:1024]} | slice | bytes 8388608 | tf_op jit(solution)/shard_map/slice | solution.py:358
  185.3 0.6 slice.78
  185.9 0.8 slice.79
  (33 shorter events, 2.5 us)
Async XLA Ops:
  0.6 10.4 %copy-start = (bf16[1024,1024]{1,0:T(8,128)(2,1)S(1)}, bf16[1024,1024]{1,0:T(8,128)(2,1)}, u32[]{:S(2)}) copy-start(bf16[1024,1024]{1,0:T(8,128)(2,1)} %param.20) | copy-start | bytes 6291460
  0.6 7.3 %copy-start.4 = (f32[64,1024]{1,0:T(8,128)S(1)}, f32[64,1024]{1,0:T(8,128)}, u32[]{:S(2)}) copy-start(f32[64,1024]{1,0:T(8,128)} %param.19) | copy-start | bytes 786436
  1.5 9.6 %copy-start.8 = (f32[1024]{0:T(1024)S(1)}, f32[1024]{0:T(1024)}, u32[]{:S(2)}) copy-start(f32[1024]{0:T(1024)} %param.21) | copy-start | bytes 12292
  11.1 9.1 %copy-start.2 = (bf16[2048,1024]{0,1:T(8,128)(2,1)}, bf16[2048,1024]{0,1:T(8,128)(2,1)S(1)}, u32[]{:S(2)}) copy-start(bf16[2048,1024]{0,1:T(8,128)(2,1)S(1)} %fusion.9) | copy-start | bytes 12582916
  11.1 11.1 %copy-start.5 = (bf16[100,1024]{1,0:T(8,128)(2,1)S(1)}, bf16[100,1024]{1,0:T(8,128)(2,1)}, u32[]{:S(2)}) copy-start(bf16[100,1024]{1,0:T(8,128)(2,1)} %param.22) | copy-start | bytes 614404
  11.1 11.1 %copy-start.6 = (f32[100]{0:T(128)S(1)}, f32[100]{0:T(128)}, u32[]{:S(2)}) copy-start(f32[100]{0:T(128)} %param.23) | copy-start | bytes 1204
  20.1 2.0 %copy-start.1 = (bf16[2048,1024]{1,0:T(8,128)(2,1)}, bf16[2048,1024]{1,0:T(8,128)(2,1)S(1)}, u32[]{:S(2)}) copy-start(bf16[2048,1024]{1,0:T(8,128)(2,1)S(1)} %get-tuple-element.47) | copy-start | bytes 12582916
  20.1 16.8 %copy-start.7 = (f32[1,1,128]{2,1,0:T(1,128)S(1)}, f32[1,1,128]{2,1,0:T(1,128)}, u32[]{:S(2)}) copy-start(f32[1,1,128]{2,1,0:T(1,128)} %param.27) | copy-start | bytes 1540
  25.5 36.2 %all-to-all-start = ((f32[100,1,2048]{0,1,2:T(1,128)}), f32[100,1,2048]{0,1,2:T(1,128)S(1)}, u32[]{:S(2)}, u32[]{:S(2)}) async-start(f32[100,1,2048]{0,1,2:T(1,128)} %copy.28), calls=%async_computation | async-start | bytes 2097152 | tf_op jit(solution)/shard_map/all_to_all | solution.py:320
  73.1 18.0 %all-to-all-start.1 = ((bf16[100,16,128]{2,0,1:T(8,128)(2,1)}), bf16[100,16,128]{2,0,1:T(8,128)(2,1)S(1)}, u32[]{:S(2)}, u32[]{:S(2)}) async-start(bf16[100,16,128]{2,0,1:T(8,128)(2,1)} %copy.30), calls=%async_computation.1 | async-start | bytes 851968 | tf_op jit(solution)/shard_map/all_to_all | solution.py:341
  94.3 9.0 %copy-start.3 = (bf16[2048,1024]{0,1:T(8,128)(2,1)S(1)}, bf16[2048,1024]{0,1:T(8,128)(2,1)}, u32[]{:S(2)}) copy-start(bf16[2048,1024]{0,1:T(8,128)(2,1)} %copy-done.2) | copy-start | bytes 12582916

commit v2 on v1

--- a/solution.py
+++ b/solution.py
@@ -248,36 +248,267 @@
     return buffers, sems
 
 
-def total_kernel(acc, out, *scratch):
+VARS_PAD = 112
+ROOT = 0.7978845608028654
+CUBE = 0.044715
+
+
+def chunk_rows(start, size):
+    return pl.ds(pl.multiple_of(start, 128), size)
+
+
+def step_kernel(
+    seed, ic, target, hidden, table, w1, b1, w2, b2, bank, weight, out,
+    noisy, noisy_t, pre, act, pred, ens, grad_send, grad_t, part_grad, acc, *rest
+):
+    buffers, sems = rest[:9], rest[9:25]
+    pred_s, pred_r, ret_s, ret_r = rest[25:]
     spot = place()
-    greet(partners(spot))
-    job = Total(spot, acc, out, *scratch[:9], scratch[9:])
-    blocks = range(BLOCKS)
-    for b in blocks:
-        job.pair_start(b)
-    for b in blocks:
-        job.pair_end(b)
-        job.first_start(b)
-    for b in blocks:
-        job.first_end(b)
-        job.second_start(b)
-    for b in blocks:
-        job.second_end(b)
+    core, x, y, z = spot
+    z_hi, z_lo = lax.div(z, 4), lax.rem(z, 4)
+    me = y * 4 + z_lo
+    others = [(t, i) for t in range(4) for i in range(4) if t + i > 0]
+
+    def member_at(t, i):
+        return lax.rem(y + t, 4) * 4 + lax.rem(z_lo + i, 4)
+
+    def member_device(member):
+        return (lax.axis_index("cuts"), member, x)
+
+    known = [member_device(member_at(t, i)) for t, i in others]
+    known += [device(1 - core, x, y, z)]
+    known += [device(core, lax.rem(x + k, 4), y, z) for k in range(1, 4)]
+    known += [device(core, x, y, (1 - z_hi) * 4 + k) for k in range(4)]
+    greet(known)
+
+    def pred_copy(t, i, source):
+        owner = member_at(t, i)
+        slot = 4 * t + i - 1
+        return pltpu.make_async_remote_copy(
+            src_ref=pred.at[owner, 0:104], dst_ref=ens.at[source, 0:104],
+            send_sem=pred_s.at[slot], recv_sem=pred_r.at[slot],
+            device_id=member_device(owner), device_id_type=MESH,
+        )
+
+    def back_copy(t, i, source):
+        owner = member_at(t, i)
+        slot = 4 * t + i - 1
+        return pltpu.make_async_remote_copy(
+            src_ref=grad_send.at[owner], dst_ref=grad_t.at[:, chunk_rows(source * 128, 128)],
+            send_sem=ret_s.at[slot], recv_sem=ret_r.at[slot],
+            device_id=member_device(owner), device_id_type=MESH,
+        )
+
+    def source_of(t, i):
+        return lax.rem(y + 4 - t, 4) * 4 + lax.rem(z_lo + 4 - i, 4)
+
+    noise = table[pl.ds(seed[0], 1), :]
+
+    for t in range(4):
+        top = lax.rem(y + t, 4) * 512
+
+        def add_noise(q, _):
+            rows = chunk_rows(top + q * 128, 128)
+            noisy[rows, :] = (hidden[rows, :].astype(jnp.float32) + noise).astype(jnp.bfloat16)
+            return 0
+
+        lax.fori_loop(0, 4, add_noise, 0)
+        rows = chunk_rows(top, 512)
+
+        def inner(n, _):
+            columns = chunk_rows(n * 256, 256)
+            v = jnp.dot(noisy[rows, :], w1[:, columns], preferred_element_type=jnp.float32) + b1[:, columns]
+            pre[rows, columns] = v
+            bend = jnp.tanh(v * (ROOT + (ROOT * CUBE) * (v * v)))
+            half = 0.5 * v
+            act[rows, columns] = (half + half * bend).astype(jnp.bfloat16)
+            return 0
+
+        lax.fori_loop(0, 4, inner, 0)
+        guess = lax.dot_general(
+            w2[...], act[rows, :], (((1,), (1,)), ((), ())), preferred_element_type=jnp.float32
+        ) + b2[...]
+        base = lax.rem(y + t, 4) * 4
+        for i in range(4):
+            pred[base + i] = guess[:, 128 * i : 128 * i + 128]
+        for i in range(4):
+            if t + i > 0:
+                pred_copy(t, i, me).start()
+    ens[me] = pred[me]
+
+    def bend_back(r, _):
+        rows = chunk_rows(r * 128, 128)
+
+        def piece(n, _):
+            columns = chunk_rows(n * 256, 256)
+            v = pre[rows, columns]
+            square = v * v
+            bend = jnp.tanh(v * (ROOT + (ROOT * CUBE) * square))
+            slope = ROOT + (3.0 * ROOT * CUBE) * square
+            pre[rows, columns] = 0.5 * ((1.0 + bend) + (v * slope) * (1.0 - bend * bend))
+            return 0
+
+        lax.fori_loop(0, 4, piece, 0)
+        return 0
+
+    lax.fori_loop(0, 16, bend_back, 0)
+
+    def turn(r, _):
+        rows = chunk_rows(r * 256, 256)
+
+        def piece(n, _):
+            columns = chunk_rows(n * 256, 256)
+            noisy_t[columns, rows] = noisy[rows, columns].T
+            return 0
+
+        lax.fori_loop(0, 4, piece, 0)
+        return 0
+
+    lax.fori_loop(0, 8, turn, 0)
+
+    for t, i in others:
+        pred_copy(t, i, me).wait_send()
+        pred_copy(t, i, source_of(t, i)).wait_recv()
+
+    epsilon = (1.0 - FAIR_ALPHA) / 16
+    pair_scale = (1.0 - epsilon) / (16 * 15.0)
+    area = weight[...]
+
+    def score(start, size):
+        rows = pl.ds(start, size)
+        first = bank[ic[0], rows, :]
+        truth = bank[target[0], rows, :]
+        values = [ens[m, rows, :] + first for m in range(16)]
+        ranks = [None] * 16
+        for a in range(16):
+            for b in range(a + 1, 16):
+                low = values[a] < values[b]
+                high = values[a] > values[b]
+                sign = jnp.where(high, 1.0, jnp.where(low, -1.0, 0.0))
+                ranks[a] = sign if ranks[a] is None else ranks[a] + sign
+                ranks[b] = -sign if ranks[b] is None else ranks[b] - sign
+        skill = jnp.zeros((size, 128), jnp.float32)
+        spread = jnp.zeros((size, 128), jnp.float32)
+        for m in range(16):
+            error = values[m] - truth
+            skill = skill + jnp.abs(error)
+            spread = spread + error * ranks[m]
+            side = jnp.where(values[m] > truth, 1.0, jnp.where(values[m] < truth, -1.0, 0.0))
+            ens[m, rows, :] = (area / 4) * (side / 16 - pair_scale * ranks[m])
+        return area * (skill / 16 - pair_scale * spread)
+
+    def score_step(s, total):
+        return total + score(pl.multiple_of(s * 8, 8), 8)
+
+    total = lax.fori_loop(0, 12, score_step, jnp.zeros((8, 128), jnp.float32))
+    total = jnp.sum(total, axis=0, keepdims=True) + jnp.sum(score(96, 4), axis=0, keepdims=True)
+    total = total / (4.0 * 8192 * 100)
+
+    inside = lax.broadcasted_iota(jnp.int32, (VARS_PAD, 128), 0) < 100
+    for t, i in [(0, 0)] + others:
+        owner = member_at(t, i)
+        value = jnp.where(inside, ens[owner], 0.0).astype(jnp.bfloat16)
+        if t + i > 0:
+            grad_send[owner] = value
+            back_copy(t, i, me).start()
+        else:
+            grad_t[:, chunk_rows(me * 128, 128)] = value
+    for t, i in others:
+        back_copy(t, i, me).wait_send()
+        back_copy(t, i, source_of(t, i)).wait_recv()
+
+    job = Total(spot, acc, out, *buffers, sems)
+    ones = jnp.ones((16, 2048), jnp.bfloat16)
+    bias_row = lax.dot_general(
+        ones, grad_t[...], (((1,), (1,)), ((), ())), preferred_element_type=jnp.float32
+    )[0:1]
+    bias_row = jnp.concatenate([bias_row, jnp.zeros((1, 16), jnp.float32)], axis=1)
+
+    def packed_row(r):
+        return (r // 32) * 288 + (r % 32) // 8 * 72 + 64
+
+    def backward(block):
+        columns = pl.ds(block * 256, 256)
+
+        def spread_back(r, bias):
+            rows = chunk_rows(r * 512, 512)
+            carried = lax.dot_general(
+                grad_t[:, rows], w2[:, columns], (((0,), (0,)), ((), ())), preferred_element_type=jnp.float32
+            )
+            value = (carried * pre[rows, columns]).astype(jnp.bfloat16)
+            part_grad[rows, :] = value
+            return bias + jnp.sum(value.astype(jnp.float32), axis=0, keepdims=True)
+
+        bias = lax.fori_loop(0, 4, spread_back, jnp.zeros((1, 256), jnp.float32))
+
+        def weights(q, _):
+            wide = jnp.dot(noisy_t[chunk_rows(q * 256, 256), :], part_grad[...], preferred_element_type=jnp.float32)
+            for c in range(4):
+                acc[pl.ds(pl.multiple_of(q * 288 + 72 * c, 8), 64), columns] = wide[64 * c : 64 * c + 64]
+            return 0
+
+        lax.fori_loop(0, 4, weights, 0)
+        second = jnp.dot(grad_t[...], act[:, columns], preferred_element_type=jnp.float32)
+        for r in range(0, VARS_PAD, 8):
+            acc[pl.ds(packed_row(r), 8), columns] = second[r : r + 8]
+        row = packed_row(112)
+        acc[pl.ds(row, 8), columns] = jnp.zeros((8, 256), jnp.float32)
+        acc[pl.ds(packed_row(120), 8), columns] = jnp.zeros((8, 256), jnp.float32)
+        acc[pl.ds(row, 1), columns] = bias
+        if block == 0:
+            acc[pl.ds(row + 1, 1), pl.ds(0, 128)] = bias_row
+            acc[pl.ds(row + 1, 1), pl.ds(128, 128)] = total
+
+    for block in range(BLOCKS):
+        backward(block)
+        job.pair_start(block)
+        if block >= 1:
+            job.pair_end(block - 1)
+            job.first_start(block - 1)
+        if block >= 2:
+            job.first_end(block - 2)
+            job.second_start(block - 2)
+        if block >= 3:
+            job.second_end(block - 3)
+    job.pair_end(3)
+    job.first_start(3)
+    job.first_end(2)
+    job.second_start(2)
+    job.first_end(3)
+    job.second_start(3)
+    job.second_end(1)
+    job.second_end(2)
+    job.second_end(3)
     job.finish()
 
 
-def all_total(acc):
-    buffers, sems = total_scratch()
+def whole_step(seed, ic, target, *arrays):
+    total_buffers, total_sems = total_scratch()
+    bf16, f32 = jnp.bfloat16, jnp.float32
+    dma = pltpu.SemaphoreType.DMA
+    vmem = pl.BlockSpec(memory_space=pltpu.VMEM)
+    smem = pl.BlockSpec(memory_space=pltpu.SMEM)
     return pl.pallas_call(
-        total_kernel,
-        out_shape=jax.ShapeDtypeStruct(acc.shape, jnp.float32),
-        in_specs=[pl.BlockSpec(memory_space=pltpu.VMEM)],
-        out_specs=pl.BlockSpec(memory_space=pltpu.VMEM),
-        scratch_shapes=buffers + sems,
+        step_kernel,
+        out_shape=jax.ShapeDtypeStruct((1152, 1024), f32),
+        in_specs=[smem] * 3 + [vmem] * 8,
+        out_specs=vmem,
+        scratch_shapes=[
+            pltpu.VMEM((2048, 1024), bf16),
+            pltpu.VMEM((1024, 2048), bf16),
+            pltpu.VMEM((2048, 1024), f32),
+            pltpu.VMEM((2048, 1024), bf16),
+            pltpu.VMEM((16, VARS_PAD, 128), f32),
+            pltpu.VMEM((16, VARS_PAD, 128), f32),
+            pltpu.VMEM((16, VARS_PAD, 128), bf16),
+            pltpu.VMEM((VARS_PAD, 2048), bf16),
+            pltpu.VMEM((2048, 256), bf16),
+            pltpu.VMEM((1152, 1024), f32),
+        ] + total_buffers + total_sems + [dma((15,)), dma((15,)), dma((15,)), dma((15,))],
         compiler_params=pltpu.CompilerParams(
-            collective_id=0, has_side_effects=True, vmem_limit_bytes=48 * 1024 * 1024
+            collective_id=0, has_side_effects=True, vmem_limit_bytes=60 * 1024 * 1024
         ),
-    )(acc)
+    )(seed, ic, target, *arrays)
 
 
 def body(
@@ -293,76 +524,27 @@
     target_index,
     area_weight,
 ):
-    members_here = hidden.shape[1]
-    points_here = hidden.shape[2]
-    hidden_width = hidden.shape[3]
     variables = output_weight.shape[0]
-    seed_ids = jnp.arange(noise_table.shape[0], dtype=jnp.int32)
-    seeds_onehot = (noise_seeds[:, None] == seed_ids[None, :]).astype(jnp.float32)
-    noise_rows = jnp.dot(
-        seeds_onehot,
+    pad = VARS_PAD - variables
+    summed = whole_step(
+        noise_seeds, ic_index, target_index,
+        hidden.reshape(2048, 1024),
         noise_table,
-        precision=lax.Precision.HIGHEST,
-        preferred_element_type=jnp.float32,
-    )
-    noisy = (hidden[0].astype(jnp.float32) + noise_rows[:, None, :]).astype(jnp.bfloat16)
-    noisy = noisy.reshape(members_here * points_here, hidden_width)
-    pre_act = jnp.dot(noisy, inner_weight, preferred_element_type=jnp.float32) + inner_bias
-    activation, gelu_back = jax.vjp(jax.nn.gelu, pre_act)
-    activation = activation.astype(jnp.bfloat16)
-    prediction = (
-        lax.dot_general(
-            output_weight, activation, (((1,), (1,)), ((), ())), preferred_element_type=jnp.float32
-        )
-        + output_bias[:, None]
-    )
-    prediction = prediction.reshape(variables, members_here, points_here)
-    point_pred = lax.all_to_all(prediction, "member", split_axis=2, concat_axis=1, tiled=True)
-    member_count = point_pred.shape[1]
-    flat_bank = state_bank[:, :, 0, 0, :]
-    ic_state = lax.dynamic_index_in_dim(flat_bank, ic_index[0], 0, keepdims=False)
-    truth_field = lax.dynamic_index_in_dim(flat_bank, target_index[0], 0, keepdims=False)
-    ensemble = point_pred + ic_state[:, None, :]
-    point_weight = area_weight[0, 0]
-    sample_count = lax.axis_size("cuts") * hidden.shape[0]
-    total_points = lax.axis_size("grid") * points_here
-    epsilon = (1.0 - FAIR_ALPHA) / member_count
-    pair_scale = (1.0 - epsilon) / (member_count * (member_count - 1.0))
-    errors = ensemble - truth_field[:, None, :]
-    differences = ensemble[:, :, None, :] - ensemble[:, None, :, :]
-    skill_sum = jnp.sum(jnp.abs(errors), axis=1)
-    spread_sum = jnp.sum(jnp.abs(differences), axis=(1, 2))
-    sign_sums = jnp.sum(jnp.sign(differences), axis=2)
-    crps_field = skill_sum / member_count - 0.5 * pair_scale * spread_sum
-    local_loss = jnp.sum(point_weight * crps_field) / (sample_count * total_points * variables)
-    member_grad = (
-        point_weight / sample_count * (jnp.sign(errors) / member_count - pair_scale * sign_sums)
-    ).astype(jnp.bfloat16)
-    returned = lax.all_to_all(member_grad, "member", split_axis=1, concat_axis=2, tiled=True)
-    returned = returned.reshape(variables, members_here * points_here)
-    grad_b2 = jnp.sum(returned.astype(jnp.float32), axis=1)
-    grad_w2 = jnp.dot(returned, activation, preferred_element_type=jnp.float32)
-    carried = lax.dot_general(
-        returned, output_weight, (((0,), (0,)), ((), ())), preferred_element_type=jnp.float32
-    )
-    pre_grad = gelu_back(carried)[0].astype(jnp.bfloat16)
-    grad_b1 = jnp.sum(pre_grad.astype(jnp.float32), axis=0)
-    grad_w1 = lax.dot_general(
-        noisy, pre_grad, (((0,), (0,)), ((), ())), preferred_element_type=jnp.float32
-    )
-    rows = jnp.zeros((28, hidden_width), jnp.float32)
-    rows = rows.at[0].set(grad_b1).at[1, :variables].set(grad_b2).at[1, variables].set(local_loss)
-    second = jnp.concatenate([grad_w2, rows], axis=0)
-    packed = jnp.concatenate([grad_w1.reshape(4, 4, 64, hidden_width), second.reshape(4, 4, 8, hidden_width)], axis=2)
-    summed = all_total(packed.reshape(1152, hidden_width)).reshape(4, 4, 72, hidden_width)
-    grad_w1 = summed[:, :, :64].reshape(hidden_width, hidden_width)
-    second = summed[:, :, 64:].reshape(128, hidden_width)
+        inner_weight,
+        inner_bias.reshape(1, 1024),
+        jnp.pad(output_weight, ((0, pad), (0, 0))),
+        jnp.pad(output_bias, (0, pad)).reshape(VARS_PAD, 1),
+        state_bank.reshape(8, variables, 128),
+        area_weight.reshape(1, 128),
+    ).reshape(4, 4, 72, 1024)
+    grad_w1 = summed[:, :, :64].reshape(1024, 1024)
+    second = summed[:, :, 64:].reshape(128, 1024)
     return (
         grad_w1,
-        second[variables],
+        second[112],
         second[:variables],
-        second[variables + 1, :variables],
-        second[variables + 1, variables],
+        second[113, :variables],
+        jnp.sum(second[113, 128:256]),
     )
 
 

time: 187 us -> 137 us (0.73)
  Pallas kernels: 66.6 us -> 121 us
  waiting for transfers between devices: 37.1 us -> 0 us
  matrix products: 28.6 us -> 0 us
  other arithmetic: 17.9 us -> 0.6 us
  starting transfers between devices: 13.6 us -> 0 us
  local copies, waits for them, and re-layouts: 19.2 us -> 12.6 us
    pallas_call x1, Pallas kernels: 66.6 us -> 121 us  [whole_step(): pl.pallas_call(step_kernel, out_shape=jax.ShapeDtypeStruct((1152, 1024),...]
    all_to_all x2 -> x0, waiting for transfers between devices: 37.1 us -> none  [the longest x1 24.8 us: body(): lax.all_to_all(prediction, 'member', split_axis=2, concat_axis=1, tiled=T...]
    dot_general x6 -> x0, matrix products: 28.6 us -> none  [the longest x1 9.02 us: body(): jnp.dot(noisy, inner_weight, preferred_element_type=jnp.float32)]
    all_to_all x2 -> x0, starting transfers between devices: 13.6 us -> none  [the longest x1 9.2 us: body(): lax.all_to_all(prediction, 'member', split_axis=2, concat_axis=1, tiled=T...]
    reduce_sum x4 -> x1, other arithmetic: 9.53 us -> 0.6 us  [body(): jnp.sum(second[113, 128:256])]
    unnamed x23 -> x0, local copies, waits for them, and re-layouts: 8.64 us -> none
    concatenate x2 -> x0, other arithmetic: 5.07 us -> none  [the longest x1 5.03 us: body(): jnp.concatenate([grad_w1.reshape(4, 4, 64, hidden_width), second.reshape(...]
    convert_element_type x2 -> x0, other arithmetic: 3.28 us -> none  [the longest x1 2.93 us: body(): (hidden[0].astype(jnp.float32) + noise_rows[:, None, :]).astype(jnp.bfloa...]
  transfers between devices with their start and end apart: 2 -> 0, of which waited for: 2 -> 0; matrix products, arithmetic and copies ran while one was open for 1% -> 0% of each run, Pallas kernels for 0% -> 0%
where the time goes in v2:
time: 137 us
  Pallas kernels  121 us (88%)
  local copies, waits for them, and re-layouts  12.6 us (9%)
  between operations  2.59 us (2%)
    pallas_call x1, Pallas kernels, whole_step(): pl.pallas_call(step_kernel, out_shape=jax.ShapeDtypeStruct((1152, 1024),...  121 us
    slice x1, local copies, waits for them, and re-layouts, body(): grad_w1 = summed[:, :, :64].reshape(1024, 1024)  4.79 us

profile of v2, /device:TPU:1, one launch (start us, length us, event | category | flops | bytes accessed | tf_op | source)
XLA Modules:
  0.0 136.6 jit_solution(4202982606764472063)
XLA Ops:
  0.6 1.8 %copy.22 = f32[8,100,1,1,128]{4,1,0,2,3:T(8,128)} copy(f32[8,100,1,1,128]{4,3,2,1,0:T(1,128)} %param.18) | data formatting | bytes 819200 | tf_op jit(solution)/shard_map/reshape | solution.py:537
  2.4 1.6 %pad.8.w2 = bf16[112,1024]{1,0:T(8,128)(2,1)} pad(bf16[100,1024]{1,0:T(8,128)(2,1)} %param.16, bf16[]{:T(256)} %constant.4.clone.1), padding=0_12x0_0 | pad | bytes 434178 | tf_op jit(solution)/shard_map/jit(_pad)/pad | solution.py:535
  4.1 0.7 pad_bitcast_fusion
  4.7 0.7 copy.18.b2
  7.4 120.9 %shard_map.146 = f32[1152,1024]{1,0:T(8,128)} custom-call(s32[1]{0:T(128)S(6)} %copy.23.seed, s32[1]{0:T(128)S(6)} %copy.24.ic, s32[1]{0:T(128)S(6)} %copy.25.target, bf16[2048,1024]{1,0:T(8,128)(2,1)} %bitcast.18, f32[64,1024]{1,0:T(8,128)} %table.1, bf16[1024,1024]{1,0:T(8,128)(2,1)} %w1.1, f32[1,1024]{1,0:T(1,128)} %bitcast.24, bf16[112,1024]{1,0:T(8,128)(2,1)} %pad.8.w2, ...), custom_call_target="tpu_custom_call" | custom-call | tf_op jit(solution)/shard_map/pallas_call | solution.py:491
  128.3 1.1 slice.25
  129.4 0.8 slice.27
  130.2 0.6 slice.26
  130.7 0.5 slice_bitcast_fusion
  131.3 0.6 slice_reduce_fusion
  131.9 4.8 %slice.24 = f32[4,4,64,1024]{3,2,1,0:T(8,128)} slice(f32[4,4,72,1024]{3,2,1,0:T(8,128)} %bitcast.16), slice={[0:4], [0:4], [0:64], [0:1024]} | slice | bytes 8388608 | tf_op jit(solution)/shard_map/slice | solution.py:540

commit v3 on v2

--- a/solution.py
+++ b/solution.py
@@ -21,15 +21,6 @@
     return (lax.div(z, 4) * 2 + core, y * 4 + lax.rem(z, 4), x)
 
 
-def partners(spot):
-    core, x, y, z = spot
-    found = [device(1 - core, x, y, z)]
-    found += [device(core, lax.rem(x + k, 4), y, z) for k in range(1, 4)]
-    found += [device(core, x, lax.rem(y + k, 4), z) for k in range(1, 4)]
-    found += [device(core, x, y, lax.rem(z + k, 8)) for k in range(1, 8)]
-    return found
-
-
 def greet(devices):
     barrier = pltpu.get_barrier_semaphore()
     for one in devices:
@@ -37,11 +28,14 @@
     pl.semaphore_wait(barrier, len(devices))
 
 
+WIRE = jnp.bfloat16
+
+
 class Total:
-    def __init__(self, spot, acc, out, pair, part1, got1, part2, got2, ztx, zrx, ztile, zall, sems):
+    def __init__(self, spot, acc, out, pair, send1, got1, part2, got2, ztx, zrx, gtx, zall, sems):
         self.spot, self.acc, self.out = spot, acc, out
-        self.pair, self.part1, self.got1, self.part2, self.got2 = pair, part1, got1, part2, got2
-        self.ztx, self.zrx, self.ztile, self.zall = ztx, zrx, ztile, zall
+        self.pair, self.send1, self.got1, self.part2, self.got2 = pair, send1, got1, part2, got2
+        self.ztx, self.zrx, self.gtx, self.zall = ztx, zrx, gtx, zall
         (self.pair_s, self.pair_r, self.s1, self.r1, self.s2, self.r2, self.zs, self.zr,
          self.gz_s, self.gz_r, self.g2_s, self.g2_r, self.g1_s, self.g1_r, self.gp_s, self.gp_r) = sems
 
@@ -74,28 +68,37 @@
         self.pair_copy(block).start()
 
     def pair_end(self, block):
-        core = self.spot[0]
+        columns = self.columns(block, self.spot[0])
         self.pair_copy(block).wait()
-        self.part1[block] = self.acc[:, self.columns(block, core)] + self.pair[block]
+
+        def add(q, _):
+            rows = pl.ds(pl.multiple_of(q * 288, 32), 288)
+            value = self.acc[rows, columns] + self.pair[block, rows]
+            self.pair[block, rows] = value
+            self.send1[block, rows] = value.astype(WIRE)
+            return 0
+
+        lax.fori_loop(0, 4, add, 0)
 
     def first_copy(self, block, k):
         mine = self.axes(block)[0]
-        rows = pl.ds(pl.multiple_of(lax.rem(mine + k, 4) * 288, 8), 288)
+        rows = pl.ds(pl.multiple_of(lax.rem(mine + k, 4) * 288, 32), 288)
         return self.copy(
-            self.part1.at[block, rows], self.got1.at[block, k - 1],
+            self.send1.at[block, rows], self.got1.at[block, k - 1],
             self.s1.at[block, k - 1], self.r1.at[block, k - 1], self.along(block, 0, k),
         )
 
     def first_start(self, block):
-        for k in range(1, 4):
+        for k in (2, 1, 3):
             self.first_copy(block, k).start()
 
     def first_end(self, block):
         mine = self.axes(block)[0]
         for k in range(1, 4):
             self.first_copy(block, k).wait()
-        own = self.part1[block, pl.ds(pl.multiple_of(mine * 288, 8), 288)]
-        self.part2[block] = (own + self.got1[block, 0]) + (self.got1[block, 1] + self.got1[block, 2])
+        own = self.pair[block, pl.ds(pl.multiple_of(mine * 288, 32), 288)]
+        got = [self.got1[block, k].astype(jnp.float32) for k in range(3)]
+        self.part2[block] = (own + got[0]) + (got[1] + got[2])
 
     def second_copy(self, block, k):
         mine = self.axes(block)[1]
@@ -106,73 +109,88 @@
         )
 
     def second_start(self, block):
-        for k in range(1, 4):
+        for k in (2, 1, 3):
             self.second_copy(block, k).start()
 
     def second_end(self, block):
         mine = self.axes(block)[1]
+        half, odd = block // 2, block % 2
         for k in range(1, 4):
             self.second_copy(block, k).wait()
         own = self.part2[block, pl.ds(pl.multiple_of(mine * 72, 8), 72)]
         total = (own + self.got2[block, 0]) + (self.got2[block, 1] + self.got2[block, 2])
         for other in range(8):
-            self.ztx[other, block, 0:8] = total[8 * other : 8 * other + 8]
-            self.ztx[other, block, 8:16] = total[64:72]
-
-    def z_copy(self, k):
+            self.ztx[half, other, 8 * odd : 8 * odd + 8] = total[8 * other : 8 * other + 8]
+            if other % 2 == odd:
+                self.ztx[half, other, 16:24] = total[64:72]
+
+    def z_copy(self, half, k):
         core, x, y, z = self.spot
         other = lax.rem(z + k, 8)
         return self.copy(
-            self.ztx.at[other], self.zrx.at[z], self.zs.at[k - 1], self.zr.at[k - 1], device(core, x, y, other)
-        )
-
-    def z_start(self):
+            self.ztx.at[half, other], self.zrx.at[half, z], self.zs.at[half, k - 1], self.zr.at[half, k - 1],
+            device(core, x, y, other),
+        )
+
+    def z_start(self, half):
         z = self.spot[3]
-        for k in range(1, 8):
-            self.z_copy(k).start()
-        self.zrx[z] = self.ztx[z]
-
-    def z_end(self):
+        for k in (4, 3, 5, 2, 6, 1, 7):
+            self.z_copy(half, k).start()
+        self.zrx[half, z] = self.ztx[half, z]
+
+    def z_end(self, half):
         core, x, y, z = self.spot
         for k in range(1, 8):
-            self.z_copy(k).wait_send()
+            self.z_copy(half, k).wait_send()
             origin = lax.rem(z + 8 - k, 8)
             self.copy(
-                self.ztx.at[z], self.zrx.at[origin], self.zs.at[k - 1], self.zr.at[k - 1], device(core, x, y, origin)
+                self.ztx.at[half, z], self.zrx.at[half, origin], self.zs.at[half, k - 1], self.zr.at[half, k - 1],
+                device(core, x, y, origin),
             ).wait_recv()
-        total = self.zrx[0]
+        total = self.zrx[half, 0]
         for other in range(1, 8):
-            total = total + self.zrx[other]
-        self.ztile[...] = total
-
-    def gather_z_copy(self, k, spot_z):
+            total = total + self.zrx[half, other]
+        tile = total[16:24]
+        rest = tile - tile.astype(jnp.bfloat16).astype(jnp.float32)
+        odd = lax.rem(z, 2)
+        one, two = (1 - odd) * x + odd * y, (1 - odd) * y + odd * x
+        row = lax.broadcasted_iota(jnp.int32, (8, 128), 0)
+        index = jnp.broadcast_to(4 * one + two, (8, 128))
+        moved = jnp.concatenate([rest[0:2], rest[0:2], rest[0:4]], axis=0)
+        tile = jnp.where((index == 14) & (row >= 2) & (row < 4), moved, tile)
+        self.gtx[half] = jnp.concatenate([total[0:16], tile, jnp.zeros((8, 128), jnp.float32)], axis=0).astype(
+            jnp.bfloat16
+        )
+
+    def gather_z_copy(self, half, k, spot_z):
         core, x, y, z = self.spot
         return self.copy(
-            self.ztile.at[:, 0:8], self.zall.at[spot_z], self.gz_s.at[k - 1], self.gz_r.at[k - 1],
+            self.gtx.at[half], self.zall.at[half, spot_z], self.gz_s.at[half, k - 1], self.gz_r.at[half, k - 1],
             device(core, x, y, lax.rem(z + k, 8)),
         )
 
-    def gather_z_start(self):
+    def gather_z_start(self, half):
         z = self.spot[3]
-        for k in range(1, 8):
-            self.gather_z_copy(k, z).start()
-        self.zall[z] = self.ztile[:, 0:8]
-
-    def chunk(self, block):
-        one, two = self.axes(block)
-        return one * 288 + two * 72
-
-    def gather_z_end(self):
+        for k in (4, 3, 5, 2, 6, 1, 7):
+            self.gather_z_copy(half, k, z).start()
+        self.zall[half, z] = self.gtx[half]
+
+    def gather_z_end(self, half):
         core, _, _, z = self.spot
         for k in range(1, 8):
-            self.gather_z_copy(k, z).wait_send()
-            self.gather_z_copy(k, lax.rem(z + 8 - k, 8)).wait_recv()
-        for block in range(BLOCKS):
-            base = self.chunk(block)
-            columns = self.columns(block, core)
-            for other in range(8):
-                self.out[pl.ds(pl.multiple_of(base + 8 * other, 8), 8), columns] = self.zall[other, block]
-            self.out[pl.ds(pl.multiple_of(base + 64, 8), 8), columns] = self.ztile[block, 8:16]
+            self.gather_z_copy(half, k, z).wait_send()
+            self.gather_z_copy(half, k, lax.rem(z + 8 - k, 8)).wait_recv()
+        parts = [self.zall[half, other].astype(jnp.float32) for other in range(8)]
+        for odd in range(2):
+            block = 2 * half + odd
+            one, two = self.axes(block)
+            whole = jnp.concatenate(
+                [part[8 * odd : 8 * odd + 8] for part in parts]
+                + [parts[odd][16:24], jnp.zeros((8, 128), jnp.float32)],
+                axis=0,
+            )
+            rows = pl.ds(pl.multiple_of(one * 320 + two * 80, 16), 80)
+            self.out[block, core, rows] = whole.astype(jnp.bfloat16)
 
     def gather_copy(self, block, phase, k, sender):
         core = self.spot[0]
@@ -180,68 +198,53 @@
         if phase == 1:
             if sender:
                 two = lax.rem(two + 4 - k, 4)
-            rows, size, send, recv = one * 288 + two * 72, 72, self.g2_s, self.g2_r
+            rows, size, send, recv = one * 320 + two * 80, 80, self.g2_s, self.g2_r
         else:
             if sender:
                 one = lax.rem(one + 4 - k, 4)
-            rows, size, send, recv = one * 288, 288, self.g1_s, self.g1_r
-        spot = self.out.at[pl.ds(pl.multiple_of(rows, 8), size), self.columns(block, core)]
+            rows, size, send, recv = one * 320, 320, self.g1_s, self.g1_r
+        spot = self.out.at[block, core, pl.ds(pl.multiple_of(rows, 16), size)]
         return self.copy(spot, spot, send.at[block, k - 1], recv.at[block, k - 1], self.along(block, phase, k))
 
-    def gather_start(self, block, phase):
-        for k in range(1, 4):
-            self.gather_copy(block, phase, k, False).start()
-
-    def gather_end(self, block, phase):
-        for k in range(1, 4):
-            self.gather_copy(block, phase, k, False).wait_send()
-            self.gather_copy(block, phase, k, True).wait_recv()
-
-    def gather_pair_copy(self, block, core_of):
+    def gather_start(self, half, phase):
+        for block in (2 * half, 2 * half + 1):
+            for k in (2, 1, 3):
+                self.gather_copy(block, phase, k, False).start()
+
+    def gather_end(self, half, phase):
+        for block in (2 * half, 2 * half + 1):
+            for k in range(1, 4):
+                self.gather_copy(block, phase, k, False).wait_send()
+                self.gather_copy(block, phase, k, True).wait_recv()
+
+    def gather_pair_copy(self, half, core_of):
         core, x, y, z = self.spot
-        spot = self.out.at[:, self.columns(block, core_of)]
-        return self.copy(spot, spot, self.gp_s.at[block], self.gp_r.at[block], device(1 - core, x, y, z))
-
-    def gather_pair_start(self, block):
-        self.gather_pair_copy(block, self.spot[0]).start()
-
-    def gather_pair_end(self, block):
-        self.gather_pair_copy(block, self.spot[0]).wait_send()
-        self.gather_pair_copy(block, 1 - self.spot[0]).wait_recv()
-
-    def finish(self):
-        blocks = range(BLOCKS)
-        self.z_start()
-        self.z_end()
-        self.gather_z_start()
-        self.gather_z_end()
-        for b in blocks:
-            self.gather_start(b, 1)
-        for b in blocks:
-            self.gather_end(b, 1)
-            self.gather_start(b, 0)
-        for b in blocks:
-            self.gather_end(b, 0)
-            self.gather_pair_start(b)
-        for b in blocks:
-            self.gather_pair_end(b)
+        spot = self.out.at[pl.ds(2 * half, 2), core_of]
+        return self.copy(spot, spot, self.gp_s.at[half], self.gp_r.at[half], device(1 - core, x, y, z))
+
+    def gather_pair_start(self, half):
+        self.gather_pair_copy(half, self.spot[0]).start()
+
+    def gather_pair_end(self, half):
+        self.gather_pair_copy(half, self.spot[0]).wait_send()
+        self.gather_pair_copy(half, 1 - self.spot[0]).wait_recv()
 
 
 def total_scratch():
-    f32 = jnp.float32
+    f32, bf16 = jnp.float32, jnp.bfloat16
     dma = pltpu.SemaphoreType.DMA
     buffers = [
         pltpu.VMEM((BLOCKS, 1152, 128), f32),
-        pltpu.VMEM((BLOCKS, 1152, 128), f32),
-        pltpu.VMEM((BLOCKS, 3, 288, 128), f32),
+        pltpu.VMEM((BLOCKS, 1152, 128), WIRE),
+        pltpu.VMEM((BLOCKS, 3, 288, 128), WIRE),
         pltpu.VMEM((BLOCKS, 288, 128), f32),
         pltpu.VMEM((BLOCKS, 3, 72, 128), f32),
-        pltpu.VMEM((8, BLOCKS, 16, 128), f32),
-        pltpu.VMEM((8, BLOCKS, 16, 128), f32),
-        pltpu.VMEM((BLOCKS, 16, 128), f32),
-        pltpu.VMEM((8, BLOCKS, 8, 128), f32),
+        pltpu.VMEM((2, 8, 24, 128), f32),
+        pltpu.VMEM((2, 8, 24, 128), f32),
+        pltpu.VMEM((2, 32, 128), bf16),
+        pltpu.VMEM((2, 8, 32, 128), bf16),
     ]
-    shapes = [(BLOCKS,), (BLOCKS, 3), (BLOCKS, 3), (7,), (7,), (BLOCKS, 3), (BLOCKS, 3), (BLOCKS,)]
+    shapes = [(BLOCKS,), (BLOCKS, 3), (BLOCKS, 3), (2, 7), (2, 7), (BLOCKS, 3), (BLOCKS, 3), (2,)]
     sems = []
     for shape in shapes:
         sems += [dma(shape), dma(shape)]
@@ -258,8 +261,9 @@
 
 
 def step_kernel(
-    seed, ic, target, hidden, table, w1, b1, w2, b2, bank, weight, out,
-    noisy, noisy_t, pre, act, pred, ens, grad_send, grad_t, part_grad, acc, *rest
+    seed, ic, target, hidden_far, table_far, w1_far, b1_far, w2_far, b2_far, bank_far, weight_far, out_far,
+    out, out_sem, table, w1, b1, w2_raw, b2, bank, weight, w2, bias_out, load_sem,
+    fresh_a, fresh_b, noisy, noisy_t, pre, act, pred, ens, grad_send, grad_t, part_grad, acc, *rest
 ):
     buffers, sems = rest[:9], rest[9:25]
     pred_s, pred_r, ret_s, ret_r = rest[25:]
@@ -279,7 +283,32 @@
     known += [device(1 - core, x, y, z)]
     known += [device(core, lax.rem(x + k, 4), y, z) for k in range(1, 4)]
     known += [device(core, x, y, (1 - z_hi) * 4 + k) for k in range(4)]
+    def load(t):
+        rows = chunk_rows(lax.rem(y + t, 4) * 512, 512)
+        return pltpu.make_async_copy(hidden_far.at[rows], noisy.at[rows], load_sem.at[t])
+
+    pairs = [(table_far, table), (w1_far, w1), (b1_far, b1), (w2_far, w2_raw), (b2_far, b2), (bank_far, bank),
+             (weight_far, weight)]
+    loads = [pltpu.make_async_copy(far, near, load_sem.at[4 + n]) for n, (far, near) in enumerate(pairs)]
+    load_table, load_w1, load_b1, load_w2, load_b2, load_bank, load_weight = loads
+    load_table.start()
+    load(0).start()
+    for one in loads[1:]:
+        one.start()
+    for t in range(1, 4):
+        load(t).start()
+    load_w2.wait()
+    load_b2.wait()
+    w2[...] = jnp.zeros_like(w2)
+    w2[0:100] = w2_raw[...]
+    bias_out[...] = jnp.zeros_like(bias_out)
+    bias_out[:, 0:100] = b2[...]
+    wide_bias = jnp.broadcast_to(bias_out[...], (VARS_PAD, 128))
+    lane = lax.broadcasted_iota(jnp.int32, (VARS_PAD, 128), 1)
+    line = lax.broadcasted_iota(jnp.int32, (VARS_PAD, 128), 0)
+    bias_column = jnp.sum(jnp.where(lane == line, wide_bias, 0.0), axis=1, keepdims=True)
     greet(known)
+    load_table.wait()
 
     def pred_copy(t, i, source):
         owner = member_at(t, i)
@@ -302,32 +331,43 @@
     def source_of(t, i):
         return lax.rem(y + 4 - t, 4) * 4 + lax.rem(z_lo + 4 - i, 4)
 
+    fresh = (fresh_a, fresh_b)
     noise = table[pl.ds(seed[0], 1), :]
 
     for t in range(4):
         top = lax.rem(y + t, 4) * 512
 
+        load(t).wait()
+
         def add_noise(q, _):
             rows = chunk_rows(top + q * 128, 128)
-            noisy[rows, :] = (hidden[rows, :].astype(jnp.float32) + noise).astype(jnp.bfloat16)
+            noisy[rows, :] = (noisy[rows, :].astype(jnp.float32) + noise).astype(jnp.bfloat16)
             return 0
 
         lax.fori_loop(0, 4, add_noise, 0)
         rows = chunk_rows(top, 512)
-
-        def inner(n, _):
-            columns = chunk_rows(n * 256, 256)
-            v = jnp.dot(noisy[rows, :], w1[:, columns], preferred_element_type=jnp.float32) + b1[:, columns]
-            pre[rows, columns] = v
-            bend = jnp.tanh(v * (ROOT + (ROOT * CUBE) * (v * v)))
-            half = 0.5 * v
-            act[rows, columns] = (half + half * bend).astype(jnp.bfloat16)
-            return 0
-
-        lax.fori_loop(0, 4, inner, 0)
+        if t == 0:
+            load_w1.wait()
+            load_b1.wait()
+
+        for n in range(5):
+            if n < 4:
+                fresh[n % 2][...] = jnp.dot(
+                    noisy[rows, :], w1[:, 256 * n : 256 * n + 256], preferred_element_type=jnp.float32
+                )
+            if n > 0:
+                columns = slice(256 * n - 256, 256 * n)
+                bias = b1[:, columns]
+                for strip in range(16):
+                    here = pl.ds(pl.multiple_of(top + 32 * strip, 32), 32)
+                    v = fresh[(n - 1) % 2][32 * strip : 32 * strip + 32] + bias
+                    pre[here, columns] = v
+                    bend = jnp.tanh(v * (ROOT + (ROOT * CUBE) * (v * v)))
+                    half = 0.5 * v
+                    act[here, columns] = (half + half * bend).astype(jnp.bfloat16)
         guess = lax.dot_general(
             w2[...], act[rows, :], (((1,), (1,)), ((), ())), preferred_element_type=jnp.float32
-        ) + b2[...]
+        ) + bias_column
         base = lax.rem(y + t, 4) * 4
         for i in range(4):
             pred[base + i] = guess[:, 128 * i : 128 * i + 128]
@@ -372,12 +412,14 @@
 
     epsilon = (1.0 - FAIR_ALPHA) / 16
     pair_scale = (1.0 - epsilon) / (16 * 15.0)
+    load_bank.wait()
+    load_weight.wait()
     area = weight[...]
 
     def score(start, size):
         rows = pl.ds(start, size)
-        first = bank[ic[0], rows, :]
-        truth = bank[target[0], rows, :]
+        first = bank[ic[0], rows, 0, 0, :]
+        truth = bank[target[0], rows, 0, 0, :]
         values = [ens[m, rows, :] + first for m in range(16)]
         ranks = [None] * 16
         for a in range(16):
@@ -441,13 +483,10 @@
 
         bias = lax.fori_loop(0, 4, spread_back, jnp.zeros((1, 256), jnp.float32))
 
-        def weights(q, _):
-            wide = jnp.dot(noisy_t[chunk_rows(q * 256, 256), :], part_grad[...], preferred_element_type=jnp.float32)
-            for c in range(4):
-                acc[pl.ds(pl.multiple_of(q * 288 + 72 * c, 8), 64), columns] = wide[64 * c : 64 * c + 64]
-            return 0
-
-        lax.fori_loop(0, 4, weights, 0)
+        wide = jnp.dot(noisy_t[...], part_grad[...], preferred_element_type=jnp.float32)
+        for c in range(16):
+            start = (c // 4) * 288 + (c % 4) * 72
+            acc[start : start + 64, columns] = wide[64 * c : 64 * c + 64]
         second = jnp.dot(grad_t[...], act[:, columns], preferred_element_type=jnp.float32)
         for r in range(0, VARS_PAD, 8):
             acc[pl.ds(packed_row(r), 8), columns] = second[r : r + 8]
@@ -472,28 +511,124 @@
             job.second_end(block - 3)
     job.pair_end(3)
     job.first_start(3)
+    job.second_end(1)
+    job.z_start(0)
     job.first_end(2)
     job.second_start(2)
     job.first_end(3)
     job.second_start(3)
-    job.second_end(1)
+    job.z_end(0)
+    job.gather_z_start(0)
     job.second_end(2)
     job.second_end(3)
-    job.finish()
+    job.z_start(1)
+    job.gather_z_end(0)
+    job.gather_start(0, 1)
+    job.z_end(1)
+    job.gather_z_start(1)
+    job.gather_end(0, 1)
+    job.gather_start(0, 0)
+    job.gather_z_end(1)
+    job.gather_start(1, 1)
+    job.gather_end(0, 0)
+    job.gather_pair_start(0)
+    job.gather_end(1, 1)
+    job.gather_start(1, 0)
+    job.gather_pair_end(0)
+    first = pl.ds(0, 2)
+    stores = [pltpu.make_async_copy(out.at[first], out_far.at[first], out_sem.at[0])]
+    stores[0].start()
+    job.gather_end(1, 0)
+    job.gather_pair_start(1)
+    last = pl.ds(2, 2)
+    stores += [pltpu.make_async_copy(out.at[last, core], out_far.at[last, core], out_sem.at[1])]
+    stores[1].start()
+    job.gather_pair_end(1)
+    stores += [pltpu.make_async_copy(out.at[last, 1 - core], out_far.at[last, 1 - core], out_sem.at[2])]
+    stores[2].start()
+    for one in stores:
+        one.wait()
+
+
+def final_kernel(summed_far, grad_w1, grad_b1, grad_w2, grad_b2, loss, summed, wide, sem, load_sem):
+    copies = []
+    loads = []
+    for c in range(4):
+        rows = pl.ds(320 * c, 320)
+        loads.append(pltpu.make_async_copy(summed_far.at[:, :, rows], summed.at[:, :, rows], load_sem.at[c]))
+        loads[-1].start()
+    for q in range(16):
+        if q % 4 == 0:
+            loads[q // 4].wait()
+        for block in range(BLOCKS):
+            for core in range(2):
+                column = slice(block * 256 + core * 128, block * 256 + core * 128 + 128)
+                tile = summed[block, core, 80 * q : 80 * q + 80].astype(jnp.float32)
+                wide[64 * q : 64 * q + 64, column] = tile[0:64]
+                if q < 12:
+                    grad_w2[8 * q : 8 * q + 8, column] = tile[64:72]
+                elif q == 12:
+                    grad_w2[96:100, column] = tile[64:68]
+                elif q == 14:
+                    grad_b1[:, column] = tile[64:65] + tile[66:67]
+                    if block == 0 and core == 0:
+                        grad_b2[...] = (tile[65:66] + tile[67:68])[:, 0:100]
+                    if block == 0 and core == 1:
+                        loss[...] = jnp.sum(tile[65:66] + tile[67:68], axis=1, keepdims=True)
+        if q % 2 == 1:
+            rows = pl.ds(64 * (q - 1), 128)
+            copies.append(pltpu.make_async_copy(wide.at[rows], grad_w1.at[rows], sem.at[q // 2]))
+            copies[-1].start()
+    for one in copies:
+        one.wait()
+
+
+def finish(summed):
+    f32 = jnp.float32
+    vmem = pl.BlockSpec(memory_space=pltpu.VMEM)
+    far = pl.BlockSpec(memory_space=pltpu.HBM)
+    shapes = [(1024, 1024), (1, 1024), (100, 1024), (1, 100), (1, 1)]
+    return pl.pallas_call(
+        final_kernel,
+        out_shape=[jax.ShapeDtypeStruct(s, f32) for s in shapes],
+        in_specs=[far],
+        out_specs=[far] + [vmem] * 4,
+        scratch_shapes=[
+            pltpu.VMEM((BLOCKS, 2, 1280, 128), jnp.bfloat16),
+            pltpu.VMEM((1024, 1024), f32),
+            pltpu.SemaphoreType.DMA((8,)),
+            pltpu.SemaphoreType.DMA((4,)),
+        ],
+        compiler_params=pltpu.CompilerParams(vmem_limit_bytes=60 * 1024 * 1024),
+    )(summed)
 
 
 def whole_step(seed, ic, target, *arrays):
     total_buffers, total_sems = total_scratch()
     bf16, f32 = jnp.bfloat16, jnp.float32
     dma = pltpu.SemaphoreType.DMA
-    vmem = pl.BlockSpec(memory_space=pltpu.VMEM)
+    far = pl.BlockSpec(memory_space=pltpu.HBM)
     smem = pl.BlockSpec(memory_space=pltpu.SMEM)
     return pl.pallas_call(
         step_kernel,
-        out_shape=jax.ShapeDtypeStruct((1152, 1024), f32),
-        in_specs=[smem] * 3 + [vmem] * 8,
-        out_specs=vmem,
+        out_shape=jax.ShapeDtypeStruct((BLOCKS, 2, 1280, 128), bf16),
+        in_specs=[smem] * 3 + [far] * 8,
+        out_specs=far,
         scratch_shapes=[
+            pltpu.VMEM((BLOCKS, 2, 1280, 128), bf16),
+            dma((3,)),
+            pltpu.VMEM((64, 1024), f32),
+            pltpu.VMEM((1024, 1024), bf16),
+            pltpu.VMEM((1, 1024), f32),
+            pltpu.VMEM((100, 1024), bf16),
+            pltpu.VMEM((1, 100), f32),
+            pltpu.VMEM((8, 100, 1, 1, 128), f32),
+            pltpu.VMEM((1, 128), f32),
+            pltpu.VMEM((VARS_PAD, 1024), bf16),
+            pltpu.VMEM((1, 128), f32),
+            dma((11,)),
+            pltpu.VMEM((512, 256), f32),
+            pltpu.VMEM((512, 256), f32),
             pltpu.VMEM((2048, 1024), bf16),
             pltpu.VMEM((1024, 2048), bf16),
             pltpu.VMEM((2048, 1024), f32),
@@ -524,28 +659,19 @@
     target_index,
     area_weight,
 ):
-    variables = output_weight.shape[0]
-    pad = VARS_PAD - variables
     summed = whole_step(
         noise_seeds, ic_index, target_index,
         hidden.reshape(2048, 1024),
         noise_table,
         inner_weight,
         inner_bias.reshape(1, 1024),
-        jnp.pad(output_weight, ((0, pad), (0, 0))),
-        jnp.pad(output_bias, (0, pad)).reshape(VARS_PAD, 1),
-        state_bank.reshape(8, variables, 128),
+        output_weight,
+        output_bias.reshape(1, 100),
+        state_bank,
         area_weight.reshape(1, 128),
-    ).reshape(4, 4, 72, 1024)
-    grad_w1 = summed[:, :, :64].reshape(1024, 1024)
-    second = summed[:, :, 64:].reshape(128, 1024)
-    return (
-        grad_w1,
-        second[112],
-        second[:variables],
-        second[113, :variables],
-        jnp.sum(second[113, 128:256]),
     )
+    grad_w1, grad_b1, grad_w2, grad_b2, loss = finish(summed)
+    return grad_w1, grad_b1.reshape(1024), grad_w2, grad_b2.reshape(100), loss.reshape(())
 
 
 def solution(mesh):

time: 137 us -> 106 us (0.77)
  Pallas kernels: 121 us -> 103 us
  local copies, waits for them, and re-layouts: 12.6 us -> 0 us
    pallas_call x1 -> x2, Pallas kernels: 121 us -> 103 us  [the longest x1 99.1 us: whole_step(): pl.pallas_call(step_kernel, out_shape=jax.ShapeDtypeStruct((BLOCKS, 2, 12...]
    slice x4 -> x0, local copies, waits for them, and re-layouts: 7.25 us -> none  [the longest x1 4.79 us: body(): grad_w1 = summed[:, :, :64].reshape(1024, 1024)]
    reshape x3 -> x0, local copies, waits for them, and re-layouts: 3.17 us -> none  [the longest x1 1.79 us: body(): state_bank.reshape(8, variables, 128)]
    pad x1 -> x0, local copies, waits for them, and re-layouts: 1.64 us -> none  [body(): jnp.pad(output_weight, ((0, pad), (0, 0)))]
where the time goes in v3:
time: 106 us
  Pallas kernels  103 us (97%)
  between operations  2.74 us (3%)
    pallas_call x1, Pallas kernels, whole_step(): pl.pallas_call(step_kernel, out_shape=jax.ShapeDtypeStruct((BLOCKS, 2, 12...  99.1 us
    pallas_call x1, Pallas kernels, finish(): pl.pallas_call(final_kernel, out_shape=[jax.ShapeDtypeStruct(s, f32) for...  3.99 us

profile of v3, /device:TPU:1, one launch (start us, length us, event | category | flops | bytes accessed | tf_op | source)
XLA Modules:
  0.0 105.9 jit_solution(8536793026712185587)
XLA Ops:
  2.6 99.1 %shard_map.146.summed_far = bf16[4,2,1280,128]{3,2,1,0:T(8,128)(2,1)} custom-call(s32[1]{0:T(128)S(6)} %copy.16.seed, s32[1]{0:T(128)S(6)} %copy.17.ic, s32[1]{0:T(128)S(6)} %copy.18.target, bf16[2048,1024]{1,0:T(8,128)(2,1)} %bitcast.7, f32[64,1024]{1,0:T(8,128)} %table_far.1, bf16[1024,1024]{1,0:T(8,128)(2,1)} %w1_far.1, f32[1,1024]{1,0:T(1,128)} %bitcast.8, ...), custom_call_target="tpu_custom_call" | custom-call | tf_op jit(solution)/shard_map/pallas_call | solution.py:612
  101.7 4.0 %shard_map.147 = (f32[1024,1024]{1,0:T(8,128)}, f32[1,1024]{1,0:T(1,128)}, f32[100,1024]{1,0:T(8,128)}, f32[1,100]{1,0:T(1,128)}, f32[1,1]{1,0:T(1,128)}) custom-call(bf16[4,2,1280,128]{3,2,1,0:T(8,128)(2,1)} %shard_map.146.summed_far), custom_call_target="tpu_custom_call" | custom-call | tf_op jit(solution)/shard_map/pallas_call | solution.py:591

commit v4 on v3

--- a/solution.py
+++ b/solution.py
@@ -25,7 +25,7 @@
     barrier = pltpu.get_barrier_semaphore()
     for one in devices:
         pl.semaphore_signal(barrier, inc=1, device_id=one, device_id_type=MESH)
-    pl.semaphore_wait(barrier, len(devices))
+    return barrier
 
 
 WIRE = jnp.bfloat16
@@ -210,24 +210,30 @@
         for block in (2 * half, 2 * half + 1):
             for k in (2, 1, 3):
                 self.gather_copy(block, phase, k, False).start()
+            if phase == 0:
+                self.gather_pair_copy(block, 0, self.spot[0]).start()
 
     def gather_end(self, half, phase):
-        for block in (2 * half, 2 * half + 1):
-            for k in range(1, 4):
+        for k in (1, 3, 2):
+            for block in (2 * half, 2 * half + 1):
+                self.gather_copy(block, phase, k, True).wait_recv()
+                if phase == 0:
+                    self.gather_pair_copy(block, k, self.spot[0]).start()
+        for k in (1, 3, 2):
+            for block in (2 * half, 2 * half + 1):
                 self.gather_copy(block, phase, k, False).wait_send()
-                self.gather_copy(block, phase, k, True).wait_recv()
-
-    def gather_pair_copy(self, half, core_of):
+
+    def gather_pair_copy(self, block, k, core_of):
         core, x, y, z = self.spot
-        spot = self.out.at[pl.ds(2 * half, 2), core_of]
-        return self.copy(spot, spot, self.gp_s.at[half], self.gp_r.at[half], device(1 - core, x, y, z))
-
-    def gather_pair_start(self, half):
-        self.gather_pair_copy(half, self.spot[0]).start()
+        one = lax.rem(self.axes(block)[0] + 4 - k, 4)
+        spot = self.out.at[block, core_of, pl.ds(pl.multiple_of(one * 320, 16), 320)]
+        return self.copy(spot, spot, self.gp_s.at[block, k], self.gp_r.at[block, k], device(1 - core, x, y, z))
 
     def gather_pair_end(self, half):
-        self.gather_pair_copy(half, self.spot[0]).wait_send()
-        self.gather_pair_copy(half, 1 - self.spot[0]).wait_recv()
+        for k in (0, 1, 3, 2):
+            for block in (2 * half, 2 * half + 1):
+                self.gather_pair_copy(block, k, self.spot[0]).wait_send()
+                self.gather_pair_copy(block, k, 1 - self.spot[0]).wait_recv()
 
 
 def total_scratch():
@@ -244,7 +250,7 @@
         pltpu.VMEM((2, 32, 128), bf16),
         pltpu.VMEM((2, 8, 32, 128), bf16),
     ]
-    shapes = [(BLOCKS,), (BLOCKS, 3), (BLOCKS, 3), (2, 7), (2, 7), (BLOCKS, 3), (BLOCKS, 3), (2,)]
+    shapes = [(BLOCKS,), (BLOCKS, 3), (BLOCKS, 3), (2, 7), (2, 7), (BLOCKS, 3), (BLOCKS, 3), (BLOCKS, 4)]
     sems = []
     for shape in shapes:
         sems += [dma(shape), dma(shape)]
@@ -260,10 +266,33 @@
     return pl.ds(pl.multiple_of(start, 128), size)
 
 
+LEVELS = 31000.0
+
+
+def encode(value):
+    line = lax.broadcasted_iota(jnp.int32, (VARS_PAD, 128), 0)
+    scale = jnp.max(jnp.abs(value), axis=0, keepdims=True) * 1.01 + 1e-30
+    scale = scale.astype(jnp.bfloat16).astype(jnp.float32)
+    size = jnp.floor(jnp.abs(value) * (LEVELS / scale) + 0.5)
+    power = jnp.floor(size * (1.0 / 128.0))
+    code = jnp.exp2(power - 125.0) * (1.0 + (size - 128.0 * power) * (1.0 / 128.0))
+    code = jnp.where(value < 0.0, -code, code)
+    return jnp.where(line == 104, jnp.broadcast_to(scale, (VARS_PAD, 128)), code).astype(jnp.bfloat16)
+
+
+def decode(coded):
+    code = coded.astype(jnp.float32)
+    scale = code[104:105]
+    size = jnp.abs(code)
+    power = jnp.floor(jnp.log(size) * 1.4426950408889634)
+    whole = jnp.floor(128.0 * (power + 124.0) + 128.0 * (size * jnp.exp2(-power)) + 0.5)
+    return jnp.where(code < 0.0, -whole, whole) * (scale * (1.0 / LEVELS))
+
+
 def step_kernel(
     seed, ic, target, hidden_far, table_far, w1_far, b1_far, w2_far, b2_far, bank_far, weight_far, out_far,
     out, out_sem, table, w1, b1, w2_raw, b2, bank, weight, w2, bias_out, load_sem,
-    fresh_a, fresh_b, noisy, noisy_t, pre, act, pred, ens, grad_send, grad_t, part_grad, acc, *rest
+    fresh_a, fresh_b, noisy_0, noisy_1, noisy_2, noisy_3, raw, noisy_t, pre, act, pred, coded, ens, grad_send, grad_t, part_a, part_b, acc, *rest
 ):
     buffers, sems = rest[:9], rest[9:25]
     pred_s, pred_r, ret_s, ret_r = rest[25:]
@@ -283,11 +312,13 @@
     known += [device(1 - core, x, y, z)]
     known += [device(core, lax.rem(x + k, 4), y, z) for k in range(1, 4)]
     known += [device(core, x, y, (1 - z_hi) * 4 + k) for k in range(4)]
+    barrier = greet(known)
+
     def load(t):
         rows = chunk_rows(lax.rem(y + t, 4) * 512, 512)
-        return pltpu.make_async_copy(hidden_far.at[rows], noisy.at[rows], load_sem.at[t])
-
-    pairs = [(table_far, table), (w1_far, w1), (b1_far, b1), (w2_far, w2_raw), (b2_far, b2), (bank_far, bank),
+        return pltpu.make_async_copy(hidden_far.at[rows], raw.at[pl.ds(512 * t, 512)], load_sem.at[t])
+
+    pairs = [(table_far, table), (w1_far, w1), (b1_far, b1), (w2_far, w2_raw), (b2_far, b2), (bank_far.at[:, :, 0, 0, :], bank),
              (weight_far, weight)]
     loads = [pltpu.make_async_copy(far, near, load_sem.at[4 + n]) for n, (far, near) in enumerate(pairs)]
     load_table, load_w1, load_b1, load_w2, load_b2, load_bank, load_weight = loads
@@ -307,23 +338,22 @@
     lane = lax.broadcasted_iota(jnp.int32, (VARS_PAD, 128), 1)
     line = lax.broadcasted_iota(jnp.int32, (VARS_PAD, 128), 0)
     bias_column = jnp.sum(jnp.where(lane == line, wide_bias, 0.0), axis=1, keepdims=True)
-    greet(known)
     load_table.wait()
 
     def pred_copy(t, i, source):
         owner = member_at(t, i)
         slot = 4 * t + i - 1
         return pltpu.make_async_remote_copy(
-            src_ref=pred.at[owner, 0:104], dst_ref=ens.at[source, 0:104],
+            src_ref=pred.at[4 * t + lax.rem(z_lo + i, 4)], dst_ref=coded.at[source],
             send_sem=pred_s.at[slot], recv_sem=pred_r.at[slot],
             device_id=member_device(owner), device_id_type=MESH,
         )
 
-    def back_copy(t, i, source):
+    def back_copy(t, i, column):
         owner = member_at(t, i)
         slot = 4 * t + i - 1
         return pltpu.make_async_remote_copy(
-            src_ref=grad_send.at[owner], dst_ref=grad_t.at[:, chunk_rows(source * 128, 128)],
+            src_ref=grad_send.at[owner], dst_ref=grad_t.at[:, chunk_rows((4 - t) % 4 * 512 + column * 128, 128)],
             send_sem=ret_s.at[slot], recv_sem=ret_r.at[slot],
             device_id=member_device(owner), device_id_type=MESH,
         )
@@ -332,49 +362,55 @@
         return lax.rem(y + 4 - t, 4) * 4 + lax.rem(z_lo + 4 - i, 4)
 
     fresh = (fresh_a, fresh_b)
+    noisy = (noisy_0, noisy_1, noisy_2, noisy_3)
+    parts = (part_a, part_b)
     noise = table[pl.ds(seed[0], 1), :]
 
+    def add_noise(t, q):
+        for strip in range(8):
+            start = 128 * q + 16 * strip
+            value = raw[512 * t + start : 512 * t + start + 16].astype(jnp.float32) + noise
+            noisy[t][start : start + 16] = value.astype(jnp.bfloat16)
+
+    load(0).wait()
+    for q in range(4):
+        add_noise(0, q)
+
     for t in range(4):
-        top = lax.rem(y + t, 4) * 512
-
-        load(t).wait()
-
-        def add_noise(q, _):
-            rows = chunk_rows(top + q * 128, 128)
-            noisy[rows, :] = (noisy[rows, :].astype(jnp.float32) + noise).astype(jnp.bfloat16)
-            return 0
-
-        lax.fori_loop(0, 4, add_noise, 0)
-        rows = chunk_rows(top, 512)
+        top = 512 * t
+        if t < 3:
+            load(t + 1).wait()
         if t == 0:
             load_w1.wait()
             load_b1.wait()
-
         for n in range(5):
             if n < 4:
                 fresh[n % 2][...] = jnp.dot(
-                    noisy[rows, :], w1[:, 256 * n : 256 * n + 256], preferred_element_type=jnp.float32
+                    noisy[t][...], w1[:, 256 * n : 256 * n + 256], preferred_element_type=jnp.float32
                 )
+                if t < 3:
+                    add_noise(t + 1, n)
             if n > 0:
                 columns = slice(256 * n - 256, 256 * n)
                 bias = b1[:, columns]
                 for strip in range(16):
-                    here = pl.ds(pl.multiple_of(top + 32 * strip, 32), 32)
+                    here = slice(top + 32 * strip, top + 32 * strip + 32)
                     v = fresh[(n - 1) % 2][32 * strip : 32 * strip + 32] + bias
                     pre[here, columns] = v
                     bend = jnp.tanh(v * (ROOT + (ROOT * CUBE) * (v * v)))
                     half = 0.5 * v
                     act[here, columns] = (half + half * bend).astype(jnp.bfloat16)
         guess = lax.dot_general(
-            w2[...], act[rows, :], (((1,), (1,)), ((), ())), preferred_element_type=jnp.float32
-        ) + bias_column
-        base = lax.rem(y + t, 4) * 4
+            w2[...], act[top : top + 512], (((1,), (1,)), ((), ())), preferred_element_type=jnp.float32
+        )
         for i in range(4):
-            pred[base + i] = guess[:, 128 * i : 128 * i + 128]
+            pred[4 * t + i] = encode(guess[:, 128 * i : 128 * i + 128])
+        if t == 0:
+            pl.semaphore_wait(barrier, len(known))
         for i in range(4):
             if t + i > 0:
                 pred_copy(t, i, me).start()
-    ens[me] = pred[me]
+    coded[me] = pred[z_lo]
 
     def bend_back(r, _):
         rows = chunk_rows(r * 128, 128)
@@ -393,23 +429,27 @@
 
     lax.fori_loop(0, 16, bend_back, 0)
 
-    def turn(r, _):
-        rows = chunk_rows(r * 256, 256)
-
-        def piece(n, _):
+    for t in range(4):
+
+        def turn(n, _):
             columns = chunk_rows(n * 256, 256)
-            noisy_t[columns, rows] = noisy[rows, columns].T
+            for r in range(2):
+                start = 512 * t + 256 * r
+                noisy_t[columns, start : start + 256] = noisy[t][256 * r : 256 * r + 256, columns].T
             return 0
 
-        lax.fori_loop(0, 4, piece, 0)
-        return 0
-
-    lax.fori_loop(0, 8, turn, 0)
+        lax.fori_loop(0, 4, turn, 0)
+    noisy_t[1024:1040] = jnp.ones((16, 2048), jnp.bfloat16)
 
     for t, i in others:
         pred_copy(t, i, me).wait_send()
         pred_copy(t, i, source_of(t, i)).wait_recv()
 
+    def open_member(m, _):
+        ens[m] = decode(coded[m]) + bias_column
+        return 0
+
+    lax.fori_loop(0, 16, open_member, 0)
     epsilon = (1.0 - FAIR_ALPHA) / 16
     pair_scale = (1.0 - epsilon) / (16 * 15.0)
     load_bank.wait()
@@ -418,8 +458,8 @@
 
     def score(start, size):
         rows = pl.ds(start, size)
-        first = bank[ic[0], rows, 0, 0, :]
-        truth = bank[target[0], rows, 0, 0, :]
+        first = bank[ic[0], rows, :]
+        truth = bank[target[0], rows, :]
         values = [ens[m, rows, :] + first for m in range(16)]
         ranks = [None] * 16
         for a in range(16):
@@ -452,102 +492,99 @@
         value = jnp.where(inside, ens[owner], 0.0).astype(jnp.bfloat16)
         if t + i > 0:
             grad_send[owner] = value
-            back_copy(t, i, me).start()
+            back_copy(t, i, z_lo).start()
         else:
-            grad_t[:, chunk_rows(me * 128, 128)] = value
+            grad_t[:, chunk_rows(z_lo * 128, 128)] = value
+
+    job = Total(spot, acc, out, *buffers, sems)
+    def packed_row(r):
+        return (r // 32) * 288 + (r % 32) // 8 * 72 + 64
+
+    def carry(block):
+        columns = slice(256 * block, 256 * block + 256)
+        for r in (0, 1, 3, 2):
+            if block == 0:
+                t = (4 - r) % 4
+                for i in range(4):
+                    if t + i > 0:
+                        back_copy(t, i, lax.rem(z_lo + 4 - i, 4)).wait_recv()
+            carried = lax.dot_general(
+                grad_t[:, 512 * r : 512 * r + 512], w2[:, columns], (((0,), (0,)), ((), ())),
+                preferred_element_type=jnp.float32,
+            )
+            for strip in range(16):
+                start = 512 * r + 32 * strip
+                value = carried[32 * strip : 32 * strip + 32] * pre[start : start + 32, columns]
+                parts[block % 2][start : start + 32] = value.astype(jnp.bfloat16)
+
+    def backward(block):
+        columns = slice(256 * block, 256 * block + 256)
+        wide = jnp.dot(noisy_t[...], parts[block % 2][...], preferred_element_type=jnp.float32)
+        for c in range(16):
+            start = (c // 4) * 288 + (c % 4) * 72
+            acc[start : start + 64, columns] = wide[64 * c : 64 * c + 64]
+        second = jnp.dot(grad_t[...], act[:, columns], preferred_element_type=jnp.float32)
+        for r in range(0, VARS_PAD, 8):
+            acc[packed_row(r) : packed_row(r) + 8, columns] = second[r : r + 8]
+        low = jnp.zeros((1, 256), jnp.float32)
+        if block == 0:
+            low = jnp.concatenate([bias_row, total], axis=1)
+        row = packed_row(112)
+        acc[row : row + 8, columns] = jnp.concatenate(
+            [wide[1024:1025], low, jnp.zeros((6, 256), jnp.float32)], axis=0
+        )
+        row = packed_row(120)
+        acc[row : row + 8, columns] = jnp.zeros((8, 256), jnp.float32)
+        if block + 1 < BLOCKS:
+            carry(block + 1)
+
+    carry(0)
     for t, i in others:
-        back_copy(t, i, me).wait_send()
-        back_copy(t, i, source_of(t, i)).wait_recv()
-
-    job = Total(spot, acc, out, *buffers, sems)
+        back_copy(t, i, z_lo).wait_send()
     ones = jnp.ones((16, 2048), jnp.bfloat16)
     bias_row = lax.dot_general(
         ones, grad_t[...], (((1,), (1,)), ((), ())), preferred_element_type=jnp.float32
     )[0:1]
     bias_row = jnp.concatenate([bias_row, jnp.zeros((1, 16), jnp.float32)], axis=1)
 
-    def packed_row(r):
-        return (r // 32) * 288 + (r % 32) // 8 * 72 + 64
-
-    def backward(block):
-        columns = pl.ds(block * 256, 256)
-
-        def spread_back(r, bias):
-            rows = chunk_rows(r * 512, 512)
-            carried = lax.dot_general(
-                grad_t[:, rows], w2[:, columns], (((0,), (0,)), ((), ())), preferred_element_type=jnp.float32
-            )
-            value = (carried * pre[rows, columns]).astype(jnp.bfloat16)
-            part_grad[rows, :] = value
-            return bias + jnp.sum(value.astype(jnp.float32), axis=0, keepdims=True)
-
-        bias = lax.fori_loop(0, 4, spread_back, jnp.zeros((1, 256), jnp.float32))
-
-        wide = jnp.dot(noisy_t[...], part_grad[...], preferred_element_type=jnp.float32)
-        for c in range(16):
-            start = (c // 4) * 288 + (c % 4) * 72
-            acc[start : start + 64, columns] = wide[64 * c : 64 * c + 64]
-        second = jnp.dot(grad_t[...], act[:, columns], preferred_element_type=jnp.float32)
-        for r in range(0, VARS_PAD, 8):
-            acc[pl.ds(packed_row(r), 8), columns] = second[r : r + 8]
-        row = packed_row(112)
-        acc[pl.ds(row, 8), columns] = jnp.zeros((8, 256), jnp.float32)
-        acc[pl.ds(packed_row(120), 8), columns] = jnp.zeros((8, 256), jnp.float32)
-        acc[pl.ds(row, 1), columns] = bias
-        if block == 0:
-            acc[pl.ds(row + 1, 1), pl.ds(0, 128)] = bias_row
-            acc[pl.ds(row + 1, 1), pl.ds(128, 128)] = total
-
+    first, last = pl.ds(0, 2), pl.ds(2, 2)
+    store_first = pltpu.make_async_copy(out.at[first], out_far.at[first], out_sem.at[0])
+    store_mine = pltpu.make_async_copy(out.at[last, core], out_far.at[last, core], out_sem.at[1])
+    store_last = pltpu.make_async_copy(out.at[last, 1 - core], out_far.at[last, 1 - core], out_sem.at[2])
     for block in range(BLOCKS):
         backward(block)
         job.pair_start(block)
         if block >= 1:
             job.pair_end(block - 1)
             job.first_start(block - 1)
-        if block >= 2:
-            job.first_end(block - 2)
-            job.second_start(block - 2)
-        if block >= 3:
-            job.second_end(block - 3)
     job.pair_end(3)
     job.first_start(3)
-    job.second_end(1)
-    job.z_start(0)
-    job.first_end(2)
-    job.second_start(2)
-    job.first_end(3)
-    job.second_start(3)
-    job.z_end(0)
-    job.gather_z_start(0)
-    job.second_end(2)
-    job.second_end(3)
-    job.z_start(1)
-    job.gather_z_end(0)
-    job.gather_start(0, 1)
-    job.z_end(1)
-    job.gather_z_start(1)
-    job.gather_end(0, 1)
-    job.gather_start(0, 0)
-    job.gather_z_end(1)
-    job.gather_start(1, 1)
+    for block in range(BLOCKS):
+        job.first_end(block)
+        job.second_start(block)
+    for half in range(2):
+        job.second_end(2 * half)
+        job.second_end(2 * half + 1)
+        job.z_start(half)
+    for half in range(2):
+        job.z_end(half)
+        job.gather_z_start(half)
+    for half in range(2):
+        job.gather_z_end(half)
+        job.gather_start(half, 1)
+    for half in range(2):
+        job.gather_end(half, 1)
+        job.gather_start(half, 0)
     job.gather_end(0, 0)
-    job.gather_pair_start(0)
-    job.gather_end(1, 1)
-    job.gather_start(1, 0)
     job.gather_pair_end(0)
-    first = pl.ds(0, 2)
-    stores = [pltpu.make_async_copy(out.at[first], out_far.at[first], out_sem.at[0])]
-    stores[0].start()
+    store_first.start()
     job.gather_end(1, 0)
-    job.gather_pair_start(1)
-    last = pl.ds(2, 2)
-    stores += [pltpu.make_async_copy(out.at[last, core], out_far.at[last, core], out_sem.at[1])]
-    stores[1].start()
+    store_mine.start()
     job.gather_pair_end(1)
-    stores += [pltpu.make_async_copy(out.at[last, 1 - core], out_far.at[last, 1 - core], out_sem.at[2])]
-    stores[2].start()
-    for one in stores:
-        one.wait()
+    store_last.start()
+    store_first.wait()
+    store_mine.wait()
+    store_last.wait()
 
 
 def final_kernel(summed_far, grad_w1, grad_b1, grad_w2, grad_b2, loss, summed, wide, sem, load_sem):
@@ -622,21 +659,27 @@
             pltpu.VMEM((1, 1024), f32),
             pltpu.VMEM((100, 1024), bf16),
             pltpu.VMEM((1, 100), f32),
-            pltpu.VMEM((8, 100, 1, 1, 128), f32),
+            pltpu.VMEM((8, 100, 128), f32),
             pltpu.VMEM((1, 128), f32),
             pltpu.VMEM((VARS_PAD, 1024), bf16),
             pltpu.VMEM((1, 128), f32),
             dma((11,)),
             pltpu.VMEM((512, 256), f32),
             pltpu.VMEM((512, 256), f32),
+            pltpu.VMEM((512, 1024), bf16),
+            pltpu.VMEM((512, 1024), bf16),
+            pltpu.VMEM((512, 1024), bf16),
+            pltpu.VMEM((512, 1024), bf16),
             pltpu.VMEM((2048, 1024), bf16),
-            pltpu.VMEM((1024, 2048), bf16),
+            pltpu.VMEM((1040, 2048), bf16),
             pltpu.VMEM((2048, 1024), f32),
             pltpu.VMEM((2048, 1024), bf16),
-            pltpu.VMEM((16, VARS_PAD, 128), f32),
+            pltpu.VMEM((16, VARS_PAD, 128), bf16),
+            pltpu.VMEM((16, VARS_PAD, 128), bf16),
             pltpu.VMEM((16, VARS_PAD, 128), f32),
             pltpu.VMEM((16, VARS_PAD, 128), bf16),
             pltpu.VMEM((VARS_PAD, 2048), bf16),
+            pltpu.VMEM((2048, 256), bf16),
             pltpu.VMEM((2048, 256), bf16),
             pltpu.VMEM((1152, 1024), f32),
         ] + total_buffers + total_sems + [dma((15,)), dma((15,)), dma((15,)), dma((15,))],

time: 106 us -> 93.6 us (0.88)
  Pallas kernels: 103 us -> 90.7 us
    pallas_call x1, Pallas kernels: 99.1 us -> 86.7 us  [whole_step(): pl.pallas_call(step_kernel, out_shape=jax.ShapeDtypeStruct((BLOCKS, 2, 12...]
where the time goes in v4:
time: 93.6 us; the launch traced here: 93.4 us
  Pallas kernels  90.7 us (97%)
  between operations  2.74 us (3%)
    pallas_call x1, Pallas kernels, whole_step(): pl.pallas_call(step_kernel, out_shape=jax.ShapeDtypeStruct((BLOCKS, 2, 12...  86.7 us
    pallas_call x1, Pallas kernels, finish(): pl.pallas_call(final_kernel, out_shape=[jax.ShapeDtypeStruct(s, f32) for...  3.99 us

profile of v4, /device:TPU:1, one launch (start us, length us, event | category | flops | bytes accessed | tf_op | source)
XLA Modules:
  0.0 93.4 jit_solution(7157870511235175595)
XLA Ops:
  2.6 86.7 %shard_map.146.summed_far = bf16[4,2,1280,128]{3,2,1,0:T(8,128)(2,1)} custom-call(s32[1]{0:T(128)S(6)} %copy.16.seed, s32[1]{0:T(128)S(6)} %copy.17.ic, s32[1]{0:T(128)S(6)} %copy.18.target, bf16[2048,1024]{1,0:T(8,128)(2,1)} %bitcast.7, f32[64,1024]{1,0:T(8,128)} %table_far.1, bf16[1024,1024]{1,0:T(8,128)(2,1)} %w1_far.1, f32[1,1024]{1,0:T(1,128)} %bitcast.8, ...), custom_call_target="tpu_custom_call" | custom-call | tf_op jit(solution)/shard_map/pallas_call | solution.py:649
  89.3 4.0 %shard_map.147 = (f32[1024,1024]{1,0:T(8,128)}, f32[1,1024]{1,0:T(1,128)}, f32[100,1024]{1,0:T(8,128)}, f32[1,100]{1,0:T(1,128)}, f32[1,1]{1,0:T(1,128)}) custom-call(bf16[4,2,1280,128]{3,2,1,0:T(8,128)(2,1)} %shard_map.146.summed_far), custom_call_target="tpu_custom_call" | custom-call | tf_op jit(solution)/shard_map/pallas_call | solution.py:628

commit v5 on v4

--- a/solution.py
+++ b/solution.py
@@ -328,16 +328,6 @@
         one.start()
     for t in range(1, 4):
         load(t).start()
-    load_w2.wait()
-    load_b2.wait()
-    w2[...] = jnp.zeros_like(w2)
-    w2[0:100] = w2_raw[...]
-    bias_out[...] = jnp.zeros_like(bias_out)
-    bias_out[:, 0:100] = b2[...]
-    wide_bias = jnp.broadcast_to(bias_out[...], (VARS_PAD, 128))
-    lane = lax.broadcasted_iota(jnp.int32, (VARS_PAD, 128), 1)
-    line = lax.broadcasted_iota(jnp.int32, (VARS_PAD, 128), 0)
-    bias_column = jnp.sum(jnp.where(lane == line, wide_bias, 0.0), axis=1, keepdims=True)
     load_table.wait()
 
     def pred_copy(t, i, source):
@@ -349,12 +339,12 @@
             device_id=member_device(owner), device_id_type=MESH,
         )
 
-    def back_copy(t, i, column):
+    def back_copy(t, i, column, start, stop):
         owner = member_at(t, i)
         slot = 4 * t + i - 1
         return pltpu.make_async_remote_copy(
-            src_ref=grad_send.at[owner], dst_ref=grad_t.at[:, chunk_rows((4 - t) % 4 * 512 + column * 128, 128)],
-            send_sem=ret_s.at[slot], recv_sem=ret_r.at[slot],
+            src_ref=grad_send.at[owner, start:stop], dst_ref=grad_t.at[start:stop, chunk_rows((4 - t) % 4 * 512 + column * 128, 128)],
+            send_sem=ret_s.at[start // 48, slot], recv_sem=ret_r.at[start // 48, slot],
             device_id=member_device(owner), device_id_type=MESH,
         )
 
@@ -400,6 +390,10 @@
                     bend = jnp.tanh(v * (ROOT + (ROOT * CUBE) * (v * v)))
                     half = 0.5 * v
                     act[here, columns] = (half + half * bend).astype(jnp.bfloat16)
+        if t == 0:
+            load_w2.wait()
+            w2[...] = jnp.zeros_like(w2)
+            w2[0:100] = w2_raw[...]
         guess = lax.dot_general(
             w2[...], act[top : top + 512], (((1,), (1,)), ((), ())), preferred_element_type=jnp.float32
         )
@@ -411,6 +405,13 @@
             if t + i > 0:
                 pred_copy(t, i, me).start()
     coded[me] = pred[z_lo]
+    load_b2.wait()
+    bias_out[...] = jnp.zeros_like(bias_out)
+    bias_out[:, 0:100] = b2[...]
+    wide_bias = jnp.broadcast_to(bias_out[...], (VARS_PAD, 128))
+    lane = lax.broadcasted_iota(jnp.int32, (VARS_PAD, 128), 1)
+    line = lax.broadcasted_iota(jnp.int32, (VARS_PAD, 128), 0)
+    bias_column = jnp.sum(jnp.where(lane == line, wide_bias, 0.0), axis=1, keepdims=True)
 
     def bend_back(r, _):
         rows = chunk_rows(r * 128, 128)
@@ -429,18 +430,6 @@
 
     lax.fori_loop(0, 16, bend_back, 0)
 
-    for t in range(4):
-
-        def turn(n, _):
-            columns = chunk_rows(n * 256, 256)
-            for r in range(2):
-                start = 512 * t + 256 * r
-                noisy_t[columns, start : start + 256] = noisy[t][256 * r : 256 * r + 256, columns].T
-            return 0
-
-        lax.fori_loop(0, 4, turn, 0)
-    noisy_t[1024:1040] = jnp.ones((16, 2048), jnp.bfloat16)
-
     for t, i in others:
         pred_copy(t, i, me).wait_send()
         pred_copy(t, i, source_of(t, i)).wait_recv()
@@ -450,6 +439,17 @@
         return 0
 
     lax.fori_loop(0, 16, open_member, 0)
+    def send_back(start, stop):
+        inside = lax.broadcasted_iota(jnp.int32, (stop - start, 128), 0) < 100 - start
+        for t, i in [(0, 0)] + others:
+            owner = member_at(t, i)
+            value = jnp.where(inside, ens[owner, start:stop], 0.0).astype(jnp.bfloat16)
+            if t + i > 0:
+                grad_send[owner, start:stop] = value
+                back_copy(t, i, z_lo, start, stop).start()
+            else:
+                grad_t[start:stop, chunk_rows(z_lo * 128, 128)] = value
+
     epsilon = (1.0 - FAIR_ALPHA) / 16
     pair_scale = (1.0 - epsilon) / (16 * 15.0)
     load_bank.wait()
@@ -482,19 +482,24 @@
     def score_step(s, total):
         return total + score(pl.multiple_of(s * 8, 8), 8)
 
-    total = lax.fori_loop(0, 12, score_step, jnp.zeros((8, 128), jnp.float32))
+    total = lax.fori_loop(0, 6, score_step, jnp.zeros((8, 128), jnp.float32))
+    send_back(0, 48)
+    total = lax.fori_loop(6, 12, score_step, total)
     total = jnp.sum(total, axis=0, keepdims=True) + jnp.sum(score(96, 4), axis=0, keepdims=True)
     total = total / (4.0 * 8192 * 100)
 
-    inside = lax.broadcasted_iota(jnp.int32, (VARS_PAD, 128), 0) < 100
-    for t, i in [(0, 0)] + others:
-        owner = member_at(t, i)
-        value = jnp.where(inside, ens[owner], 0.0).astype(jnp.bfloat16)
-        if t + i > 0:
-            grad_send[owner] = value
-            back_copy(t, i, z_lo).start()
-        else:
-            grad_t[:, chunk_rows(z_lo * 128, 128)] = value
+    send_back(48, VARS_PAD)
+    for t in range(4):
+
+        def turn(n, _):
+            columns = chunk_rows(n * 256, 256)
+            for r in range(2):
+                start = 512 * t + 256 * r
+                noisy_t[columns, start : start + 256] = noisy[t][256 * r : 256 * r + 256, columns].T
+            return 0
+
+        lax.fori_loop(0, 4, turn, 0)
+    noisy_t[1024:1040] = jnp.ones((16, 2048), jnp.bfloat16)
 
     job = Total(spot, acc, out, *buffers, sems)
     def packed_row(r):
@@ -507,7 +512,8 @@
                 t = (4 - r) % 4
                 for i in range(4):
                     if t + i > 0:
-                        back_copy(t, i, lax.rem(z_lo + 4 - i, 4)).wait_recv()
+                        back_copy(t, i, lax.rem(z_lo + 4 - i, 4), 0, 48).wait_recv()
+                        back_copy(t, i, lax.rem(z_lo + 4 - i, 4), 48, VARS_PAD).wait_recv()
             carried = lax.dot_general(
                 grad_t[:, 512 * r : 512 * r + 512], w2[:, columns], (((0,), (0,)), ((), ())),
                 preferred_element_type=jnp.float32,
@@ -540,7 +546,8 @@
 
     carry(0)
     for t, i in others:
-        back_copy(t, i, z_lo).wait_send()
+        back_copy(t, i, z_lo, 0, 48).wait_send()
+        back_copy(t, i, z_lo, 48, VARS_PAD).wait_send()
     ones = jnp.ones((16, 2048), jnp.bfloat16)
     bias_row = lax.dot_general(
         ones, grad_t[...], (((1,), (1,)), ((), ())), preferred_element_type=jnp.float32
@@ -590,13 +597,13 @@
 def final_kernel(summed_far, grad_w1, grad_b1, grad_w2, grad_b2, loss, summed, wide, sem, load_sem):
     copies = []
     loads = []
-    for c in range(4):
-        rows = pl.ds(320 * c, 320)
+    for c in range(8):
+        rows = pl.ds(160 * c, 160)
         loads.append(pltpu.make_async_copy(summed_far.at[:, :, rows], summed.at[:, :, rows], load_sem.at[c]))
         loads[-1].start()
     for q in range(16):
-        if q % 4 == 0:
-            loads[q // 4].wait()
+        if q % 2 == 0:
+            loads[q // 2].wait()
         for block in range(BLOCKS):
             for core in range(2):
                 column = slice(block * 256 + core * 128, block * 256 + core * 128 + 128)
@@ -634,7 +641,7 @@
             pltpu.VMEM((BLOCKS, 2, 1280, 128), jnp.bfloat16),
             pltpu.VMEM((1024, 1024), f32),
             pltpu.SemaphoreType.DMA((8,)),
-            pltpu.SemaphoreType.DMA((4,)),
+            pltpu.SemaphoreType.DMA((8,)),
         ],
         compiler_params=pltpu.CompilerParams(vmem_limit_bytes=60 * 1024 * 1024),
     )(summed)
@@ -682,7 +689,7 @@
             pltpu.VMEM((2048, 256), bf16),
             pltpu.VMEM((2048, 256), bf16),
             pltpu.VMEM((1152, 1024), f32),
-        ] + total_buffers + total_sems + [dma((15,)), dma((15,)), dma((15,)), dma((15,))],
+        ] + total_buffers + total_sems + [dma((15,)), dma((15,)), dma((2, 15)), dma((2, 15))],
         compiler_params=pltpu.CompilerParams(
             collective_id=0, has_side_effects=True, vmem_limit_bytes=60 * 1024 * 1024
         ),

time: 93.6 us -> 92.3 us (0.986)
  Pallas kernels: 90.7 us -> 89.4 us
    pallas_call x1, Pallas kernels: 86.7 us -> 85.5 us  [whole_step(): pl.pallas_call(step_kernel, out_shape=jax.ShapeDtypeStruct((BLOCKS, 2, 12...]
where the time goes in v5:
time: 92.3 us; the launch traced here: 92.1 us
  Pallas kernels  89.4 us (97%)
  between operations  2.74 us (3%)
    pallas_call x1, Pallas kernels, whole_step(): pl.pallas_call(step_kernel, out_shape=jax.ShapeDtypeStruct((BLOCKS, 2, 12...  85.5 us
    pallas_call x1, Pallas kernels, finish(): pl.pallas_call(final_kernel, out_shape=[jax.ShapeDtypeStruct(s, f32) for...  3.91 us

profile of v5, /device:TPU:1, one launch (start us, length us, event | category | flops | bytes accessed | tf_op | source)
XLA Modules:
  0.0 92.1 jit_solution(7058711233850560054)
XLA Ops:
  2.6 85.5 %shard_map.146.summed_far = bf16[4,2,1280,128]{3,2,1,0:T(8,128)(2,1)} custom-call(s32[1]{0:T(128)S(6)} %copy.16.seed, s32[1]{0:T(128)S(6)} %copy.17.ic, s32[1]{0:T(128)S(6)} %copy.18.target, bf16[2048,1024]{1,0:T(8,128)(2,1)} %bitcast.7, f32[64,1024]{1,0:T(8,128)} %table_far.1, bf16[1024,1024]{1,0:T(8,128)(2,1)} %w1_far.1, f32[1,1024]{1,0:T(1,128)} %bitcast.8, ...), custom_call_target="tpu_custom_call" | custom-call | tf_op jit(solution)/shard_map/pallas_call | solution.py:656
  88.1 3.9 %shard_map.147 = (f32[1024,1024]{1,0:T(8,128)}, f32[1,1024]{1,0:T(1,128)}, f32[100,1024]{1,0:T(8,128)}, f32[1,100]{1,0:T(1,128)}, f32[1,1]{1,0:T(1,128)}) custom-call(bf16[4,2,1280,128]{3,2,1,0:T(8,128)(2,1)} %shard_map.146.summed_far), custom_call_target="tpu_custom_call" | custom-call | tf_op jit(solution)/shard_map/pallas_call | solution.py:635
